TPU v7x, 32 devices: a whole 2x2x4 slice. The times are simulated.
32 devices in a mesh: grp: 2 (over x), tm: 8 (over z, y), bus: 2 (over core).
Axes of the slice: x: 2, y: 2, z: 4, core: 2. Of those that a mesh axis runs over, the one named last changes fastest.
Arguments:
- network: float32 [2048, 2048], P('bus'), may hold values from -0.125 to 0.125
- upper_bound: float32 [2048], P('bus'), may hold values from 0.5 to 2
- build_cost: float32 [2048], P('bus'), may hold values from 0.5 to 8
- unit_cost: float32 [512, 2048], P(('grp', 'tm'), 'bus'), parts along dimension 0, may hold values from -6 to 6
- demand: float32 [512, 2048], P(('grp', 'tm'), 'bus'), parts along dimension 0, may hold values from -6 to 6
- inflow: float32 [4096], P(('grp', 'bus')), parts along dimension 0, may hold values from 0.05 to 1
- primal_start: float32 [512, 2048], P(('grp', 'tm'), 'bus'), parts along dimension 0, may hold values from 0 to 1
- network_start: float32 [512, 2048], P(('grp', 'tm'), 'bus'), parts along dimension 0, may hold values from 0 to 1
- energy_start: float32 [512, 2048], P(('grp', 'tm'), 'bus'), parts along dimension 0, may hold values from 0 to 1
- build_start: float32 [4096], P(('grp', 'bus')), parts along dimension 0, may hold values from 0 to 2
- accepted: int32 [16], P('grp'), parts along dimension 0, may hold values from 0 to 1
- restarts: int32 [16], P('grp'), parts along dimension 0, may hold values from 0 to 1
Outputs:
- primal_final: float32 [512, 2048], P(('grp', 'tm'), 'bus'), parts along dimension 0
- network_final: float32 [512, 2048], P(('grp', 'tm'), 'bus'), parts along dimension 0
- energy_final: float32 [512, 2048], P(('grp', 'tm'), 'bus'), parts along dimension 0
- build_final: float32 [4096], P(('grp', 'bus')), parts along dimension 0
There are 2 independent parts, one for each index of `grp`. A program takes and returns all parts, laid end to end along the dimension named above; an argument that names none is the same for every part. Nothing has to cross between parts.
Inputs may be any that keep to these rules, and one draw needn't show every extreme that they name: `accepted`: A flag, 0 or 1, for each iteration after the first. `restarts`: A flag, 0 or 1, for each iteration after the first.
All inputs are finite; a program needn't handle non-finite values.
Results may differ from a plain program's by a relative error of at most 0.00013.
Values sent between devices are 32-bit elements; how exact they have to be, the bound alone decides.
No kernel may reach another device: no remote copies, remote signals or barrier semaphores. Data moves between devices by JAX's collectives and lax.ppermute only.
A program may use at most 128 MiB of HBM per device.

v0:
```python
import jax
import jax.numpy as jnp
from jax import lax
from jax.sharding import PartitionSpec as P

ITERS = 9
MEM = 5


primal_step = 0.3
dual_step = 0.3
highest = lax.Precision.HIGHEST


def carried_in(value, axis, join, neutral, backward):
    count, mine = (lax.axis_size(axis), lax.axis_index(axis))
    pieces = lax.all_gather(value, axis)
    if backward:
        pieces = pieces[::-1]
        mine = count - 1 - mine
    subtotal = jnp.full_like(value, 0) + jnp.asarray(neutral, value.dtype)

    def step(position, subtotal):
        longer = join(subtotal, pieces[position])
        return jnp.where(position < mine, longer, subtotal)

    return lax.fori_loop(0, count - 1, step, subtotal)


def add_terms(earlier, later):
    return earlier + later


def solve_small(matrix, vector):
    size_n = vector.shape[0]
    entries = [[matrix[i, j] for j in range(size_n)] for i in range(size_n)]
    values = [vector[i] for i in range(size_n)]
    for p in range(size_n):
        for i in range(p + 1, size_n):
            factor = entries[i][p] / entries[p][p]
            for j in range(p, size_n):
                entries[i][j] = entries[i][j] - factor * entries[p][j]
            values[i] = values[i] - factor * values[p]
    result = [values[0]] * size_n
    for i in range(size_n - 1, -1, -1):
        running_value = values[i]
        for j in range(i + 1, size_n):
            running_value = running_value - entries[i][j] * result[j]
        result[i] = running_value / entries[i][i]
    return jnp.stack(result)


def mixing_weights(gram_matrix, right_side, active):
    column_count = right_side.shape[0]
    active_pairs = active[:, None] * active[None, :]
    trace_sum = jnp.sum(jnp.diagonal(gram_matrix) * active)
    shift_amount = 0.001 * trace_sum / column_count + 1e-06
    system = (
        gram_matrix * active_pairs
        + jnp.diag(1.0 - active)
        + shift_amount * jnp.eye(column_count, dtype=jnp.float32)
    )
    return solve_small(system, right_side * active) * active


def on_device(
    network,
    upper_bound,
    build_cost,
    unit_cost,
    demand,
    inflow,
    primal_start,
    network_start,
    energy_start,
    build_start,
    accepted,
    restarts,
):
    position = lax.axis_index("tm")
    local_hours = primal_start.shape[0]
    hour_iota = lax.iota(jnp.int32, local_hours)
    weight = (1.0 / (position * local_hours + hour_iota + 1).astype(jnp.float32))[:, None]
    lower_ones = (hour_iota[:, None] >= hour_iota[None, :]).astype(jnp.float32)
    upper_ones = (hour_iota[:, None] <= hour_iota[None, :]).astype(jnp.float32)
    own_build = (position == 0).astype(jnp.float32)

    def advance(primal, net_dual, energy_dual, build_level):
        scaled = energy_dual * weight
        local_tail = jnp.dot(upper_ones, scaled, precision=highest)
        block_total = local_tail[0]
        later = carried_in(block_total, "tm", add_terms, jnp.zeros_like(block_total), True)
        column_total = lax.psum(block_total, "tm")
        pulled = lax.psum_scatter(
            jnp.dot(net_dual, network, precision=highest), "bus", scatter_dimension=1, tiled=True
        )
        remaining = local_tail + later
        next_primal = jnp.clip(
            primal - primal_step * (unit_cost - pulled + remaining), 0.0, upper_bound
        )
        next_build = jnp.maximum(build_level - primal_step * (build_cost - column_total), 0.0)
        bar_primal = 2.0 * next_primal - primal
        bar_build = 2.0 * next_build - build_level
        local_run = jnp.dot(lower_ones, bar_primal, precision=highest)
        pushed = jnp.zeros_like(bar_primal) + lax.dot_general(
            lax.all_gather(bar_primal, "bus", axis=1, tiled=True),
            network,
            (((1,), (1,)), ((), ())),
            precision=highest,
        )
        earlier = carried_in(local_run[-1], "tm", add_terms, jnp.zeros_like(local_run[-1]), False)
        running = local_run + earlier
        next_net = jnp.maximum(net_dual + dual_step * (demand - pushed), 0.0)
        next_energy = jnp.maximum(
            energy_dual + dual_step * (-inflow - (bar_build - running) * weight), 0.0
        )
        return (next_primal, next_net, next_energy, next_build)

    def inner_local(first, second):
        subtotal = (
            jnp.sum(first[0] * second[0])
            + jnp.sum(first[1] * second[1])
            + jnp.sum(first[2] * second[2])
        )
        return subtotal + own_build * jnp.sum(first[3] * second[3])

    state = (primal_start, network_start, energy_start, build_start)
    totals = tuple((jnp.zeros_like(member) for member in state))
    counter = jnp.zeros((), jnp.float32)
    delta_maps = []
    delta_resid = []
    active = []
    pair_rows = []
    last_map = state
    last_resid = state
    restart_flag = jnp.zeros((), jnp.float32)
    for iteration in range(ITERS):
        if iteration > 0:
            restart_flag = restarts[iteration - 1].astype(jnp.float32)
            state = tuple(
                (
                    restart_flag * (summed / counter) + (1.0 - restart_flag) * member
                    for summed, member in zip(totals, state)
                )
            )
            totals = tuple(((1.0 - restart_flag) * summed for summed in totals))
            counter = (1.0 - restart_flag) * counter
        mapped = advance(*state)
        residual = tuple((m - z for m, z in zip(mapped, state)))
        if iteration == 0:
            following = mapped
        else:
            keep_flag = 1.0 - restart_flag
            active = [old_flag * keep_flag for old_flag in active] + [keep_flag]
            delta_maps.append(tuple((m - z for m, z in zip(mapped, last_map))))
            delta_resid.append(tuple((m - z for m, z in zip(residual, last_resid))))
            if len(delta_resid) > MEM:
                delta_maps.pop(0)
                delta_resid.pop(0)
                active.pop(0)
                pair_rows.pop(0)
                pair_rows = [entry_row[1:] for entry_row in pair_rows]
            size_n = len(delta_resid)
            newest = delta_resid[-1]
            local_row = jnp.stack([inner_local(column, newest) for column in delta_resid])
            local_right = jnp.stack([inner_local(column, residual) for column in delta_resid])
            summed_row, summed_right = lax.psum((local_row, local_right), ("tm", "bus"))
            pair_rows.append([summed_row[i] for i in range(size_n)])
            gram_matrix = jnp.stack(
                [
                    jnp.stack([pair_rows[max(i, j)][min(i, j)] for j in range(size_n)])
                    for i in range(size_n)
                ]
            )
            mix_weights = mixing_weights(gram_matrix, summed_right, jnp.stack(active))
            accept_flag = accepted[iteration - 1].astype(jnp.float32)
            following = []
            for b in range(4):
                correction = jnp.zeros_like(mapped[b])
                for j in range(size_n):
                    correction = correction + mix_weights[j] * delta_maps[j][b]
                following.append(mapped[b] - accept_flag * correction)
            following = tuple(following)
        last_map = mapped
        last_resid = residual
        state = following
        totals = tuple((summed + member for summed, member in zip(totals, state)))
        counter = counter + 1.0
    primal, net_dual, energy_dual, build_level = state
    return (primal, net_dual, energy_dual, build_level)


def solution(mesh):
    return jax.shard_map(
        on_device,
        mesh=mesh,
        in_specs=(
            P("bus", None),
            P("bus"),
            P("bus"),
            P(("grp", "tm"), "bus"),
            P(("grp", "tm"), "bus"),
            P(("grp", "bus")),
            P(("grp", "tm"), "bus"),
            P(("grp", "tm"), "bus"),
            P(("grp", "tm"), "bus"),
            P(("grp", "bus")),
            P("grp"),
            P("grp"),
        ),
        out_specs=(
            P(("grp", "tm"), "bus"),
            P(("grp", "tm"), "bus"),
            P(("grp", "tm"), "bus"),
            P(("grp", "bus")),
        ),
        check_vma=False,
    )
```

profile of v0, /device:TPU:0, one launch (start us, length us, event | category | flops | bytes accessed | tf_op | source)
XLA Modules:
  0.0 1945.2 jit_solution(17868983211393199228)
XLA Ops:
  7.3 9.2 fusion.134
  18.3 32.2 %all-gather = f32[8,1,1024]{2,1,0:T(1,128)S(1)} all-gather(f32[1,1,1024]{2,1,0:T(1,128)S(1)} %get-tuple-element.2306), channel_id=1, replica_groups=mesh['grp'=2,'tm'=8,'bus'=2] {'tm'}, dimensions={0}, use_global_device_ids=true | all-gather | bytes 36864 | tf_op jit(solution)/shard_map/all_gather | solution.py:17
  52.3 21.4 %psum.175 = f32[1024]{0:T(1024)S(1)} all-reduce(f32[1024]{0:T(1024)S(1)} %bitcast.632), channel_id=1, replica_groups=mesh['grp'=2,'tm'=8,'bus'=2] {'tm'}, use_global_device_ids=true, to_apply=%region_4.5 | all-reduce | flops 1024 | bytes 8192 | tf_op jit(solution)/shard_map/psum | solution.py:93
  89.8 30.4 %all-gather.1 = f32[8,1,1024]{2,1,0:T(1,128)S(1)} all-gather(f32[1,1,1024]{2,1,0:T(1,128)S(1)} %slice_bitcast_fusion.8), channel_id=1, replica_groups=mesh['grp'=2,'tm'=8,'bus'=2] {'tm'}, dimensions={0}, use_global_device_ids=true | all-gather | bytes 36864 | tf_op jit(solution)/shard_map/all_gather | solution.py:17
  121.0 30.4 %all-gather.2 = f32[8,1,1024]{2,1,0:T(1,128)S(1)} all-gather(f32[1,1,1024]{2,1,0:T(1,128)S(1)} %get-tuple-element.2304), channel_id=1, replica_groups=mesh['grp'=2,'tm'=8,'bus'=2] {'tm'}, dimensions={0}, use_global_device_ids=true | all-gather | bytes 36864 | tf_op jit(solution)/shard_map/all_gather | solution.py:17
  151.6 10.0 fusion.2
  161.6 7.9 fusion.47
  169.9 17.1 psum.176
  192.2 30.9 %all-gather.3 = f32[8,1,1024]{2,1,0:T(1,128)S(1)} all-gather(f32[1,1,1024]{2,1,0:T(1,128)S(1)} %slice_bitcast_fusion.7), channel_id=1, replica_groups=mesh['grp'=2,'tm'=8,'bus'=2] {'tm'}, dimensions={0}, use_global_device_ids=true | all-gather | bytes 36864 | tf_op jit(solution)/shard_map/all_gather | solution.py:17
  224.1 10.7 multiply_reduce_fusion.175
  239.5 31.1 %all-reduce.7 = (f32[1]{0:T(128)}, f32[1]{0:T(128)}) all-reduce(f32[1]{0:T(128)} %bitcast.15, f32[1]{0:T(128)} %bitcast.18), channel_id=1, replica_groups=mesh['grp'=2,'tm'=8,'bus'=2] {'tm','bus'}, use_global_device_ids=true, to_apply=%region_16.17 | all-reduce | flops 2 | bytes 16 | tf_op jit(solution)/shard_map/psum | solution.py:167
  272.9 30.4 %all-gather.4 = f32[8,1,1024]{2,1,0:T(1,128)S(1)} all-gather(f32[1,1,1024]{2,1,0:T(1,128)S(1)} %get-tuple-element.2302), channel_id=1, replica_groups=mesh['grp'=2,'tm'=8,'bus'=2] {'tm'}, dimensions={0}, use_global_device_ids=true | all-gather | bytes 36864 | tf_op jit(solution)/shard_map/all_gather | solution.py:17
  303.5 7.8 fusion.135
  311.8 17.1 psum.179
  335.6 30.4 %all-gather.5 = f32[8,1,1024]{2,1,0:T(1,128)S(1)} all-gather(f32[1,1,1024]{2,1,0:T(1,128)S(1)} %slice_bitcast_fusion.6), channel_id=1, replica_groups=mesh['grp'=2,'tm'=8,'bus'=2] {'tm'}, dimensions={0}, use_global_device_ids=true | all-gather | bytes 36864 | tf_op jit(solution)/shard_map/all_gather | solution.py:17
  366.4 11.3 multiply_reduce_fusion.166
  387.3 29.5 %all-reduce.6 = (f32[2]{0:T(128)S(1)}, f32[2]{0:T(128)S(1)}) all-reduce(f32[2]{0:T(128)S(1)} %pad_maximum_fusion.3, f32[2]{0:T(128)S(1)} %pad_maximum_fusion.5), channel_id=1, replica_groups=mesh['grp'=2,'tm'=8,'bus'=2] {'tm','bus'}, use_global_device_ids=true, to_apply=%region_36.37 | all-reduce | flops 4 | bytes 32 | tf_op jit(solution)/shard_map/psum | solution.py:167
  430.8 30.6 %all-gather.6 = f32[8,1,1024]{2,1,0:T(1,128)S(1)} all-gather(f32[1,1,1024]{2,1,0:T(1,128)S(1)} %get-tuple-element.2300), channel_id=1, replica_groups=mesh['grp'=2,'tm'=8,'bus'=2] {'tm'}, dimensions={0}, use_global_device_ids=true | all-gather | bytes 36864 | tf_op jit(solution)/shard_map/all_gather | solution.py:17
  473.7 17.1 psum.182
  501.7 30.4 %all-gather.7 = f32[8,1,1024]{2,1,0:T(1,128)S(1)} all-gather(f32[1,1,1024]{2,1,0:T(1,128)S(1)} %slice_bitcast_fusion.5), channel_id=1, replica_groups=mesh['grp'=2,'tm'=8,'bus'=2] {'tm'}, dimensions={0}, use_global_device_ids=true | all-gather | bytes 36864 | tf_op jit(solution)/shard_map/all_gather | solution.py:17
  533.2 11.3 multiply_reduce_fusion.151
  561.2 29.5 %all-reduce.5 = (f32[3]{0:T(128)S(1)}, f32[3]{0:T(128)S(1)}) all-reduce(f32[3]{0:T(128)S(1)} %pad_maximum_fusion.6, f32[3]{0:T(128)S(1)} %pad_maximum_fusion.8), channel_id=1, replica_groups=mesh['grp'=2,'tm'=8,'bus'=2] {'tm','bus'}, use_global_device_ids=true, to_apply=%region_65.66 | all-reduce | flops 6 | bytes 48 | tf_op jit(solution)/shard_map/psum | solution.py:167
  618.2 30.4 %all-gather.8 = f32[8,1,1024]{2,1,0:T(1,128)S(1)} all-gather(f32[1,1,1024]{2,1,0:T(1,128)S(1)} %get-tuple-element.2298), channel_id=1, replica_groups=mesh['grp'=2,'tm'=8,'bus'=2] {'tm'}, dimensions={0}, use_global_device_ids=true | all-gather | bytes 36864 | tf_op jit(solution)/shard_map/all_gather | solution.py:17
  652.3 7.8 fusion.137
  660.2 8.4 while.260
  668.6 17.1 psum.185
  701.4 30.8 %all-gather.9 = f32[8,1,1024]{2,1,0:T(1,128)S(1)} all-gather(f32[1,1,1024]{2,1,0:T(1,128)S(1)} %slice_bitcast_fusion.4), channel_id=1, replica_groups=mesh['grp'=2,'tm'=8,'bus'=2] {'tm'}, dimensions={0}, use_global_device_ids=true | all-gather | bytes 36864 | tf_op jit(solution)/shard_map/all_gather | solution.py:17
  732.1 8.5 while.261
  740.6 12.3 multiply_reduce_fusion.130
  774.4 29.5 %all-reduce.4 = (f32[4]{0:T(128)S(1)}, f32[4]{0:T(128)S(1)}) all-reduce(f32[4]{0:T(128)S(1)} %pad_maximum_fusion.9, f32[4]{0:T(128)S(1)} %pad_maximum_fusion.11), channel_id=1, replica_groups=mesh['grp'=2,'tm'=8,'bus'=2] {'tm','bus'}, use_global_device_ids=true, to_apply=%region_102.103 | all-reduce | flops 8 | bytes 64 | tf_op jit(solution)/shard_map/psum | solution.py:167
  845.1 30.4 %all-gather.10 = f32[8,1,1024]{2,1,0:T(1,128)S(1)} all-gather(f32[1,1,1024]{2,1,0:T(1,128)S(1)} %get-tuple-element.2296), channel_id=1, replica_groups=mesh['grp'=2,'tm'=8,'bus'=2] {'tm'}, dimensions={0}, use_global_device_ids=true | all-gather | bytes 36864 | tf_op jit(solution)/shard_map/all_gather | solution.py:17
  880.0 18.5 while.262
  903.6 7.9 fusion.138
  911.6 17.7 psum.188
  952.5 30.8 %all-gather.11 = f32[8,1,1024]{2,1,0:T(1,128)S(1)} all-gather(f32[1,1,1024]{2,1,0:T(1,128)S(1)} %slice_bitcast_fusion.3), channel_id=1, replica_groups=mesh['grp'=2,'tm'=8,'bus'=2] {'tm'}, dimensions={0}, use_global_device_ids=true | all-gather | bytes 36864 | tf_op jit(solution)/shard_map/all_gather | solution.py:17
  984.0 18.3 while.263
  1002.3 12.5 multiply_reduce_fusion.91
  1039.3 29.5 %all-reduce.3 = (f32[5]{0:T(128)S(1)}, f32[5]{0:T(128)S(1)}) all-reduce(f32[5]{0:T(128)S(1)} %stack.721, f32[5]{0:T(128)S(1)} %stack.733), channel_id=1, replica_groups=mesh['grp'=2,'tm'=8,'bus'=2] {'tm','bus'}, use_global_device_ids=true, to_apply=%region_147.148 | all-reduce | flops 10 | bytes 80 | tf_op jit(solution)/shard_map/psum | solution.py:167
  1126.7 30.4 %all-gather.12 = f32[8,1,1024]{2,1,0:T(1,128)S(1)} all-gather(f32[1,1,1024]{2,1,0:T(1,128)S(1)} %get-tuple-element.2294), channel_id=1, replica_groups=mesh['grp'=2,'tm'=8,'bus'=2] {'tm'}, dimensions={0}, use_global_device_ids=true | all-gather | bytes 36864 | tf_op jit(solution)/shard_map/all_gather | solution.py:17
  1164.3 7.9 fusion.139
  1172.2 13.5 while.264
  1187.0 17.1 psum.191
  1223.3 30.6 %all-gather.13 = f32[8,1,1024]{2,1,0:T(1,128)S(1)} all-gather(f32[1,1,1024]{2,1,0:T(1,128)S(1)} %slice_bitcast_fusion.2), channel_id=1, replica_groups=mesh['grp'=2,'tm'=8,'bus'=2] {'tm'}, dimensions={0}, use_global_device_ids=true | all-gather | bytes 36864 | tf_op jit(solution)/shard_map/all_gather | solution.py:17
  1254.5 13.5 while.265
  1268.0 12.5 multiply_reduce_fusion.61
  1304.5 29.5 %all-reduce.2 = (f32[5]{0:T(128)S(1)}, f32[5]{0:T(128)S(1)}) all-reduce(f32[5]{0:T(128)S(1)} %stack.755, f32[5]{0:T(128)S(1)} %stack.767), channel_id=1, replica_groups=mesh['grp'=2,'tm'=8,'bus'=2] {'tm','bus'}, use_global_device_ids=true, to_apply=%region_196.197 | all-reduce | flops 10 | bytes 80 | tf_op jit(solution)/shard_map/psum | solution.py:167
  1392.9 30.4 %all-gather.14 = f32[8,1,1024]{2,1,0:T(1,128)S(1)} all-gather(f32[1,1,1024]{2,1,0:T(1,128)S(1)} %get-tuple-element.2292), channel_id=1, replica_groups=mesh['grp'=2,'tm'=8,'bus'=2] {'tm'}, dimensions={0}, use_global_device_ids=true | all-gather | bytes 36864 | tf_op jit(solution)/shard_map/all_gather | solution.py:17
  1432.6 7.9 fusion.140
  1440.6 13.5 while.266
  1455.4 17.8 psum.194
  1493.3 30.6 %all-gather.15 = f32[8,1,1024]{2,1,0:T(1,128)S(1)} all-gather(f32[1,1,1024]{2,1,0:T(1,128)S(1)} %slice_bitcast_fusion.1), channel_id=1, replica_groups=mesh['grp'=2,'tm'=8,'bus'=2] {'tm'}, dimensions={0}, use_global_device_ids=true | all-gather | bytes 36864 | tf_op jit(solution)/shard_map/all_gather | solution.py:17
  1524.5 13.6 while.267
  1538.2 12.5 multiply_reduce_fusion.31
  1575.9 29.5 %all-reduce.1 = (f32[5]{0:T(128)S(1)}, f32[5]{0:T(128)S(1)}) all-reduce(f32[5]{0:T(128)S(1)} %stack.789, f32[5]{0:T(128)S(1)} %stack.801), channel_id=1, replica_groups=mesh['grp'=2,'tm'=8,'bus'=2] {'tm','bus'}, use_global_device_ids=true, to_apply=%region_245.246 | all-reduce | flops 10 | bytes 80 | tf_op jit(solution)/shard_map/psum | solution.py:167
  1657.9 8.1 multiply_add_fusion
  1666.9 30.4 %all-gather.16 = f32[8,1,1024]{2,1,0:T(1,128)S(1)} all-gather(f32[1,1,1024]{2,1,0:T(1,128)S(1)} %get-tuple-element.2290), channel_id=1, replica_groups=mesh['grp'=2,'tm'=8,'bus'=2] {'tm'}, dimensions={0}, use_global_device_ids=true | all-gather | bytes 36864 | tf_op jit(solution)/shard_map/all_gather | solution.py:17
  1697.5 8.4 while.268
  1705.9 8.0 multiply_add_fusion.1
  1714.0 7.8 fusion.141
  1721.9 17.3 psum.197
  1762.8 30.8 %all-gather.17 = f32[8,1,1024]{2,1,0:T(1,128)S(1)} all-gather(f32[1,1,1024]{2,1,0:T(1,128)S(1)} %slice_bitcast_fusion), channel_id=1, replica_groups=mesh['grp'=2,'tm'=8,'bus'=2] {'tm'}, dimensions={0}, use_global_device_ids=true | all-gather | bytes 36864 | tf_op jit(solution)/shard_map/all_gather | solution.py:17
  1793.6 8.5 while.269
  1802.1 11.0 fusion.84
  1840.1 29.5 %all-reduce = (f32[5]{0:T(128)S(1)}, f32[5]{0:T(128)S(1)}) all-reduce(f32[5]{0:T(128)S(1)} %stack.823, f32[5]{0:T(128)S(1)} %stack.835), channel_id=1, replica_groups=mesh['grp'=2,'tm'=8,'bus'=2] {'tm','bus'}, use_global_device_ids=true, to_apply=%region_294.295 | all-reduce | flops 10 | bytes 80 | tf_op jit(solution)/shard_map/psum | solution.py:167
  (746 shorter events, 450.5 us)
Async XLA Ops:
  7.2 144.4 %copy-start.13 = (f32[32,1024]{1,0:T(8,128)S(1)}, f32[32,1024]{1,0:T(8,128)}, u32[]{:S(2)}) copy-start(f32[32,1024]{1,0:T(8,128)} %param.55) | copy-start | bytes 393220
  7.2 43.8 %copy-start.73 = (s32[8]{0:T(128)S(1)}, s32[8]{0:T(128)}, u32[]{:S(2)}) copy-start(s32[8]{0:T(128)} %param.59) | copy-start | bytes 100
  7.2 66.4 %copy-start.84 = (f32[1024]{0:T(1024)S(1)}, f32[1024]{0:T(1024)}, u32[]{:S(2)}) copy-start(f32[1024]{0:T(1024)} %param.53) | copy-start | bytes 12292
  7.2 67.0 %copy-start.74 = (s32[8]{0:T(128)S(1)}, s32[8]{0:T(128)}, u32[]{:S(2)}) copy-start(s32[8]{0:T(128)} %param.58) | copy-start | bytes 100
  7.2 79.3 %copy-start.79 = (f32[1024]{0:T(1024)S(1)}, f32[1024]{0:T(1024)}, u32[]{:S(2)}) copy-start(f32[1024]{0:T(1024)} %param.57) | copy-start | bytes 12292
  7.2 79.3 %copy-start.54 = (f32[1024]{0:T(1024)S(1)}, f32[1024]{0:T(1024)}, u32[]{:S(2)}) copy-start(f32[1024]{0:T(1024)} %param.50) | copy-start | bytes 12292
  7.2 79.3 %copy-start.45 = (f32[32,1024]{1,0:T(8,128)S(1)}, f32[32,1024]{1,0:T(8,128)}, u32[]{:S(2)}) copy-start(f32[32,1024]{1,0:T(8,128)} %param.54) | copy-start | bytes 393220
  7.2 79.3 %copy-start.1 = (f32[32,1024]{1,0:T(8,128)S(1)}, f32[32,1024]{1,0:T(8,128)}, u32[]{:S(2)}) copy-start(f32[32,1024]{1,0:T(8,128)} %param.51) | copy-start | bytes 393220
  7.3 79.3 %copy-start.55 = (f32[1024]{0:T(1024)S(1)}, f32[1024]{0:T(1024)}, u32[]{:S(2)}) copy-start(f32[1024]{0:T(1024)} %param.49) | copy-start | bytes 12292
  7.3 144.3 %copy-start = (f32[32,1024]{1,0:T(8,128)S(1)}, f32[32,1024]{1,0:T(8,128)}, u32[]{:S(2)}) copy-start(f32[32,1024]{1,0:T(8,128)} %param.52) | copy-start | bytes 393220
  7.3 79.3 %reduce-scatter.10.cloned.1.call-start = ((), (), s32[]{:S(2)}) async-start(), calls=%async_computation.9 | async-start | bytes 393216 | tf_op jit(solution)/shard_map/reduce_scatter | solution.py:94
  16.6 172.4 %reduce-scatter.12.cloned.1.call-start = ((), (), s32[]{:S(2)}) async-start(), calls=%async_computation.10 | async-start | bytes 393216 | tf_op jit(solution)/shard_map/reduce_scatter | solution.py:94
  17.9 412.5 %copy-start.56 = (f32[32]{0:T(128)}, f32[32]{0:T(128)S(1)}, u32[]{:S(2)}) copy-start(f32[32]{0:T(128)S(1)} %convert_divide_fusion) | copy-start | bytes 388
  169.5 162.9 %reduce-scatter.14.cloned.1.call-start = ((), (), s32[]{:S(2)}) async-start(), calls=%async_computation.11 | async-start | bytes 393216 | tf_op jit(solution)/shard_map/reduce_scatter | solution.py:94
  187.7 303.1 %copy-start.65 = (f32[1024]{0:T(1024)}, f32[1024]{0:T(1024)S(1)}, u32[]{:S(2)}) copy-start(f32[1024]{0:T(1024)S(1)} %get-tuple-element.2278) | copy-start | bytes 12292
  189.0 239.4 %copy-start.57 = (f32[1024]{0:T(1024)}, f32[1024]{0:T(1024)S(1)}, u32[]{:S(2)}) copy-start(f32[1024]{0:T(1024)S(1)} %multiply_subtract_fusion.44) | copy-start | bytes 12292
  311.4 185.2 %reduce-scatter.16.cloned.1.call-start = ((), (), s32[]{:S(2)}) async-start(), calls=%async_computation.12 | async-start | bytes 393216 | tf_op jit(solution)/shard_map/reduce_scatter | solution.py:94
  329.7 142.2 %copy-start.70 = (f32[1024]{0:T(1024)}, f32[1024]{0:T(1024)S(1)}, u32[]{:S(2)}) copy-start(f32[1024]{0:T(1024)S(1)} %get-tuple-element.2262) | copy-start | bytes 12292
  329.7 161.1 %copy-start.63 = (f32[1024]{0:T(1024)}, f32[1024]{0:T(1024)S(1)}, u32[]{:S(2)}) copy-start(f32[1024]{0:T(1024)S(1)} %get-tuple-element.2264) | copy-start | bytes 12292
  329.7 161.1 %copy-start.64 = (f32[1024]{0:T(1024)}, f32[1024]{0:T(1024)S(1)}, u32[]{:S(2)}) copy-start(f32[1024]{0:T(1024)S(1)} %get-tuple-element.2260) | copy-start | bytes 12292
  416.8 84.9 %copy-start.77 = (f32[2]{0:T(128)}, f32[2]{0:T(128)S(1)}, u32[]{:S(2)}) copy-start(f32[2]{0:T(128)S(1)} %get-tuple-element.2111) | copy-start | bytes 28
  471.8 223.5 %reduce-scatter.18.cloned.1.call-start = ((), (), s32[]{:S(2)}) async-start(), calls=%async_computation.13 | async-start | bytes 393216 | tf_op jit(solution)/shard_map/reduce_scatter | solution.py:94
  492.1 40.5 %copy-start.69 = (f32[1024]{0:T(1024)}, f32[1024]{0:T(1024)S(1)}, u32[]{:S(2)}) copy-start(f32[1024]{0:T(1024)S(1)} %get-tuple-element.2235) | copy-start | bytes 12292
  499.5 195.8 %copy-start.9 = (f32[32,1024]{1,0:T(8,128)}, f32[32,1024]{1,0:T(8,128)S(1)}, u32[]{:S(2)}) copy-start(f32[32,1024]{1,0:T(8,128)S(1)} %get-tuple-element.2246) | copy-start | bytes 393220
  499.5 45.0 %copy-start.49 = (f32[32,1024]{1,0:T(8,128)S(1)}, f32[32,1024]{1,0:T(8,128)}, u32[]{:S(2)}) copy-start(f32[32,1024]{1,0:T(8,128)} %get-tuple-element.2247) | copy-start | bytes 393220
  544.5 150.8 %copy-start.19 = (f32[32,1024]{1,0:T(8,128)}, f32[32,1024]{1,0:T(8,128)S(1)}, u32[]{:S(2)}) copy-start(f32[32,1024]{1,0:T(8,128)S(1)} %get-tuple-element.2555) | copy-start | bytes 393220
  550.4 98.3 %copy-start.27 = (f32[32,1024]{1,0:T(8,128)}, f32[32,1024]{1,0:T(8,128)S(1)}, u32[]{:S(2)}) copy-start(f32[32,1024]{1,0:T(8,128)S(1)} %get-tuple-element.2240) | copy-start | bytes 393220
  660.1 288.0 %reduce-scatter.20.cloned.1.call-start = ((), (), s32[]{:S(2)}) async-start(), calls=%async_computation.14 | async-start | bytes 393216 | tf_op jit(solution)/shard_map/reduce_scatter | solution.py:94
  699.0 111.2 %copy-start.7 = (f32[32,1024]{1,0:T(8,128)}, f32[32,1024]{1,0:T(8,128)S(1)}, u32[]{:S(2)}) copy-start(f32[32,1024]{1,0:T(8,128)S(1)} %get-tuple-element.2219) | copy-start | bytes 393220
  699.0 142.9 %copy-start.23 = (f32[32,1024]{1,0:T(8,128)S(1)}, f32[32,1024]{1,0:T(8,128)}, u32[]{:S(2)}) copy-start(f32[32,1024]{1,0:T(8,128)} %get-tuple-element.2256) | copy-start | bytes 393220
  699.2 41.4 %copy-start.40 = (f32[32,1024]{1,0:T(8,128)}, f32[32,1024]{1,0:T(8,128)S(1)}, u32[]{:S(2)}) copy-start(f32[32,1024]{1,0:T(8,128)S(1)} %fusion.67) | copy-start | bytes 393220
  701.4 51.6 %copy-start.53 = (f32[32,1024]{1,0:T(8,128)S(1)}, f32[32,1024]{1,0:T(8,128)}, u32[]{:S(2)}) copy-start(f32[32,1024]{1,0:T(8,128)} %get-tuple-element.2220) | copy-start | bytes 393220
  803.9 34.4 %copy-start.76 = (f32[4]{0:T(128)}, f32[4]{0:T(128)S(1)}, u32[]{:S(2)}) copy-start(f32[4]{0:T(128)S(1)} %get-tuple-element.2107) | copy-start | bytes 52
  843.5 58.4 %copy-start.29 = (f32[32,1024]{1,0:T(8,128)}, f32[32,1024]{1,0:T(8,128)S(1)}, u32[]{:S(2)}) copy-start(f32[32,1024]{1,0:T(8,128)S(1)} %get-tuple-element.2199) | copy-start | bytes 393220
  844.5 54.0 %copy-start.37 = (f32[32,1024]{1,0:T(8,128)}, f32[32,1024]{1,0:T(8,128)S(1)}, u32[]{:S(2)}) copy-start(f32[32,1024]{1,0:T(8,128)S(1)} %fusion.33) | copy-start | bytes 393220
  903.6 40.4 %copy-start.16 = (f32[32,1024]{1,0:T(8,128)}, f32[32,1024]{1,0:T(8,128)S(1)}, u32[]{:S(2)}) copy-start(f32[32,1024]{1,0:T(8,128)S(1)} %get-tuple-element.2195) | copy-start | bytes 393220
  911.5 304.5 %reduce-scatter.22.cloned.1.call-start = ((), (), s32[]{:S(2)}) async-start(), calls=%async_computation.15 | async-start | bytes 393216 | tf_op jit(solution)/shard_map/reduce_scatter | solution.py:94
  1014.8 201.2 %copy-start.3 = (f32[32,1024]{1,0:T(8,128)S(1)}, f32[32,1024]{1,0:T(8,128)}, u32[]{:S(2)}) copy-start(f32[32,1024]{1,0:T(8,128)} %get-tuple-element.2192) | copy-start | bytes 393220
  1037.8 230.2 %copy-start.2 = (f32[32,1024]{1,0:T(8,128)S(1)}, f32[32,1024]{1,0:T(8,128)}, u32[]{:S(2)}) copy-start(f32[32,1024]{1,0:T(8,128)} %get-tuple-element.2187) | copy-start | bytes 393220
  1164.3 51.8 %copy-start.14 = (f32[32,1024]{1,0:T(8,128)}, f32[32,1024]{1,0:T(8,128)S(1)}, u32[]{:S(2)}) copy-start(f32[32,1024]{1,0:T(8,128)S(1)} %get-tuple-element.2171) | copy-start | bytes 393220
  1172.2 313.8 %reduce-scatter.24.cloned.1.call-start = ((), (), s32[]{:S(2)}) async-start(), calls=%async_computation.16 | async-start | bytes 393216 | tf_op jit(solution)/shard_map/reduce_scatter | solution.py:94
  1209.1 45.3 %copy-start.66 = (f32[1024]{0:T(1024)}, f32[1024]{0:T(1024)S(1)}, u32[]{:S(2)}) copy-start(f32[1024]{0:T(1024)S(1)} %get-tuple-element.2155) | copy-start | bytes 12292
  1220.9 206.9 %copy-start.6 = (f32[32,1024]{1,0:T(8,128)S(1)}, f32[32,1024]{1,0:T(8,128)}, u32[]{:S(2)}) copy-start(f32[32,1024]{1,0:T(8,128)} %get-tuple-element.2196) | copy-start | bytes 393220
  1280.5 205.5 %copy-start.5 = (f32[32,1024]{1,0:T(8,128)S(1)}, f32[32,1024]{1,0:T(8,128)}, u32[]{:S(2)}) copy-start(f32[32,1024]{1,0:T(8,128)} %get-tuple-element.2190) | copy-start | bytes 393220
  1286.0 200.0 %copy-start.30 = (f32[32,1024]{1,0:T(8,128)}, f32[32,1024]{1,0:T(8,128)S(1)}, u32[]{:S(2)}) copy-start(f32[32,1024]{1,0:T(8,128)S(1)} %get-tuple-element.2161) | copy-start | bytes 393220
  1390.7 37.1 %copy-start.32 = (f32[32,1024]{1,0:T(8,128)}, f32[32,1024]{1,0:T(8,128)S(1)}, u32[]{:S(2)}) copy-start(f32[32,1024]{1,0:T(8,128)S(1)} %get-tuple-element.2151) | copy-start | bytes 393220
  1432.6 53.3 %copy-start.17 = (f32[32,1024]{1,0:T(8,128)}, f32[32,1024]{1,0:T(8,128)S(1)}, u32[]{:S(2)}) copy-start(f32[32,1024]{1,0:T(8,128)S(1)} %get-tuple-element.2149) | copy-start | bytes 393220
  1440.6 314.5 %reduce-scatter.26.cloned.1.call-start = ((), (), s32[]{:S(2)}) async-start(), calls=%async_computation.17 | async-start | bytes 393216 | tf_op jit(solution)/shard_map/reduce_scatter | solution.py:94
  1478.4 46.1 %copy-start.67 = (f32[1024]{0:T(1024)}, f32[1024]{0:T(1024)S(1)}, u32[]{:S(2)}) copy-start(f32[1024]{0:T(1024)S(1)} %get-tuple-element.2134) | copy-start | bytes 12292
  1486.0 171.9 %copy-start.8 = (f32[32,1024]{1,0:T(8,128)S(1)}, f32[32,1024]{1,0:T(8,128)}, u32[]{:S(2)}) copy-start(f32[32,1024]{1,0:T(8,128)} %get-tuple-element.2200) | copy-start | bytes 393220
  1490.9 215.0 %copy-start.18 = (f32[32,1024]{1,0:T(8,128)S(1)}, f32[32,1024]{1,0:T(8,128)}, u32[]{:S(2)}) copy-start(f32[32,1024]{1,0:T(8,128)} %get-tuple-element.2558) | copy-start | bytes 393220
  1491.1 47.0 %copy-start.43 = (f32[32,1024]{1,0:T(8,128)}, f32[32,1024]{1,0:T(8,128)S(1)}, u32[]{:S(2)}) copy-start(f32[32,1024]{1,0:T(8,128)S(1)} %fusion.64) | copy-start | bytes 393220
  1557.1 198.0 %copy-start.25 = (f32[32,1024]{1,0:T(8,128)}, f32[32,1024]{1,0:T(8,128)S(1)}, u32[]{:S(2)}) copy-start(f32[32,1024]{1,0:T(8,128)S(1)} %get-tuple-element.2139) | copy-start | bytes 393220
  1666.9 39.0 %copy-start.36 = (f32[32,1024]{1,0:T(8,128)}, f32[32,1024]{1,0:T(8,128)S(1)}, u32[]{:S(2)}) copy-start(f32[32,1024]{1,0:T(8,128)S(1)} %fusion.27) | copy-start | bytes 393220
  1705.9 49.1 %copy-start.59 = (f32[1024]{0:T(1024)S(1)}, f32[1024]{0:T(1024)}, u32[]{:S(2)}) copy-start(f32[1024]{0:T(1024)} %get-tuple-element.1442) | copy-start | bytes 12292
  1721.8 92.2 %copy-start.12 = (f32[32,1024]{1,0:T(8,128)S(1)}, f32[32,1024]{1,0:T(8,128)}, u32[]{:S(2)}) copy-start(f32[32,1024]{1,0:T(8,128)} %get-tuple-element.2193) | copy-start | bytes 393220
  1721.8 92.3 %copy-start.35 = (f32[32,1024]{1,0:T(8,128)S(1)}, f32[32,1024]{1,0:T(8,128)}, u32[]{:S(2)}) copy-start(f32[32,1024]{1,0:T(8,128)} %get-tuple-element.2169) | copy-start | bytes 393220
  1721.8 94.0 %copy-start.15 = (f32[32,1024]{1,0:T(8,128)S(1)}, f32[32,1024]{1,0:T(8,128)}, u32[]{:S(2)}) copy-start(f32[32,1024]{1,0:T(8,128)} %get-tuple-element.2162) | copy-start | bytes 393220
  1721.8 97.9 %copy-start.10 = (f32[32,1024]{1,0:T(8,128)S(1)}, f32[32,1024]{1,0:T(8,128)}, u32[]{:S(2)}) copy-start(f32[32,1024]{1,0:T(8,128)} %get-tuple-element.2182) | copy-start | bytes 393220
  1721.8 97.9 %copy-start.33 = (f32[32,1024]{1,0:T(8,128)S(1)}, f32[32,1024]{1,0:T(8,128)}, u32[]{:S(2)}) copy-start(f32[32,1024]{1,0:T(8,128)} %get-tuple-element.2159) | copy-start | bytes 393220
  1755.0 164.3 %copy-start.22 = (f32[32,1024]{1,0:T(8,128)S(1)}, f32[32,1024]{1,0:T(8,128)}, u32[]{:S(2)}) copy-start(f32[32,1024]{1,0:T(8,128)} %get-tuple-element.2146) | copy-start | bytes 393220
  1760.3 163.7 %copy-start.24 = (f32[32,1024]{1,0:T(8,128)S(1)}, f32[32,1024]{1,0:T(8,128)}, u32[]{:S(2)}) copy-start(f32[32,1024]{1,0:T(8,128)} %get-tuple-element.2152) | copy-start | bytes 393220
  1760.3 163.7 %copy-start.26 = (f32[32,1024]{1,0:T(8,128)S(1)}, f32[32,1024]{1,0:T(8,128)}, u32[]{:S(2)}) copy-start(f32[32,1024]{1,0:T(8,128)} %copy-done.25) | copy-start | bytes 393220
  1762.8 170.6 %copy-start.28 = (f32[32,1024]{1,0:T(8,128)S(1)}, f32[32,1024]{1,0:T(8,128)}, u32[]{:S(2)}) copy-start(f32[32,1024]{1,0:T(8,128)} %get-tuple-element.2150) | copy-start | bytes 393220
  (30 other events, 387.6 us)
Sparse Core Ops, SparseCore 0:
  16.7 10.3 reduce-scatter.9
  169.6 4.9 reduce-scatter.11
  311.5 4.8 reduce-scatter.13
  471.9 4.9 reduce-scatter.15
  660.3 4.8 reduce-scatter.17
  911.7 4.9 reduce-scatter.19
  1172.3 4.8 reduce-scatter.21
  1440.7 4.9 reduce-scatter.23
  1722.0 4.8 reduce-scatter.25
where the time goes:
time: 1970 us; the launch traced here: 1950 us
  blocking collectives  967 us (49%)
  between operations  362 us (18%)
  other arithmetic  316 us (16%)
  matrix products  184 us (9%)
  local copies, waits for them, and re-layouts  113 us (6%)
    all_gather x18, blocking collectives, carried_in(): pieces = lax.all_gather(value, axis)  551 us
    psum x8, blocking collectives, on_device(): summed_row, summed_right = lax.psum((local_row, local_right), ('tm', 'bus'))  237 us
    psum x9, blocking collectives, advance(): column_total = lax.psum(block_total, 'tm')  160 us
    dot_general x9, matrix products, advance(): lax.dot_general(lax.all_gather(bar_primal, 'bus', axis=1, tiled=True), ne...  104 us
    select_n x126, other arithmetic, step(): return jnp.where(position < mine, longer, subtotal)  83.9 us
    dot_general x9, matrix products, advance(): jnp.dot(net_dual, network, precision=highest)  72.1 us
    add x14, other arithmetic, on_device(): restart_flag * (summed / counter) + (1.0 - restart_flag) * member  50.1 us
    dynamic_slice x126, local copies, waits for them, and re-layouts, step(): longer = join(subtotal, pieces[position])  41.1 us
  transfers between devices with their start and end apart: 9, of which 0 were waited for; matrix products, arithmetic and copies ran while one was open for 5% of the time, Pallas kernels for 0%

commit v1 on v0

v1 whole, which is shorter than its diff:
```python
from types import SimpleNamespace as Space

import jax
import jax.numpy as jnp
from jax import lax
from jax.experimental import pallas as pl
from jax.experimental.pallas import tpu as pltpu
from jax.sharding import PartitionSpec as P

ITERS = 9
MEM = 5
LANES = 128
ROWS = 16
LIMIT = 10 * 1024 * 1024
X, Y, E, U, SLOPE, COLUMN = range(6)

primal_step = 0.3
dual_step = 0.3
f32 = jnp.float32
bf16 = jnp.bfloat16


def shape(*dims, dtype=f32):
    return jax.ShapeDtypeStruct(dims, dtype)


def run(body, ins, outs):
    in_leaves, in_tree = jax.tree.flatten(ins)
    out_leaves, out_tree = jax.tree.flatten(outs)

    def kernel(*refs):
        given = jax.tree.unflatten(in_tree, refs[: len(in_leaves)])
        made = jax.tree.unflatten(out_tree, refs[len(in_leaves) :])
        body(Space(**given), Space(**made))

    def place(leaf):
        return pl.BlockSpec(memory_space=pltpu.SMEM if leaf.dtype == jnp.int32 else pltpu.VMEM)

    results = pl.pallas_call(
        kernel,
        out_shape=out_leaves,
        in_specs=[place(leaf) for leaf in in_leaves],
        out_specs=[place(leaf) for leaf in out_leaves],
        compiler_params=pltpu.CompilerParams(vmem_limit_bytes=LIMIT),
        name=body.__name__,
    )(*in_leaves)
    return Space(**jax.tree.unflatten(out_tree, results))


def lane_blocks(width):
    return [slice(j * LANES, (j + 1) * LANES) for j in range(width // LANES)]


def row_iota(rows):
    return lax.broadcasted_iota(jnp.int32, (rows, LANES), 0)


def running_sum(block):
    rows = block.shape[0]
    at = row_iota(rows)
    step = 1
    while step < rows:
        block = block + jnp.where(at >= step, pltpu.roll(block, step, 0), 0.0)
        step *= 2
    return block


def tail_sum(block):
    rows = block.shape[0]
    at = row_iota(rows)
    step = 1
    while step < rows:
        block = block + jnp.where(at < rows - step, pltpu.roll(block, rows - step, 0), 0.0)
        step *= 2
    return block


def to_tile(block):
    rows = block.shape[0]
    total = block[0:8]
    for i in range(8, rows, 8):
        total = total + block[i : i + 8]
    return total


def product(left, high, low, transposed):
    rows = left.shape[0]
    dims = (((1,), (1 if transposed else 0,)), ((), ()))
    left_high = left.astype(bf16)
    left_low = (left - left_high.astype(f32)).astype(bf16)
    both = lax.dot_general(
        jnp.concatenate([left_high, left_low], axis=0), high, dims, preferred_element_type=f32
    )
    rest = lax.dot_general(left_high, low, dims, preferred_element_type=f32)
    return both[:rows] + (both[rows:] + rest)


def split_network(network, bus):
    rows, units = network.shape
    width = units // 2
    step = min(128, rows)

    def kernel(_, own, other, own_high, own_low, other_high, other_low):
        for source, high, low in ((own, own_high, own_low), (other, other_high, other_low)):
            value = source[...]
            rounded = value.astype(bf16)
            high[...] = rounded
            low[...] = (value - rounded.astype(f32)).astype(bf16)

    part = pl.BlockSpec((step, width), lambda i, b: (i, 0))
    return pl.pallas_call(
        kernel,
        out_shape=[shape(rows, width, dtype=bf16)] * 4,
        grid_spec=pltpu.PrefetchScalarGridSpec(
            num_scalar_prefetch=1,
            grid=(rows // step,),
            in_specs=[
                pl.BlockSpec((step, width), lambda i, b: (i, b[0])),
                pl.BlockSpec((step, width), lambda i, b: (i, 1 - b[0])),
            ],
            out_specs=[part] * 4,
        ),
        compiler_params=pltpu.CompilerParams(vmem_limit_bytes=LIMIT),
    )(bus, network, network)


def solve_rows(entries, values):
    size_n = len(values)
    entries = [list(row) for row in entries]
    values = list(values)
    for p in range(size_n):
        for i in range(p + 1, size_n):
            factor = entries[i][p] / entries[p][p]
            for j in range(p + 1, size_n):
                entries[i][j] = entries[i][j] - factor * entries[p][j]
            values[i] = values[i] - factor * values[p]
    result = [None] * size_n
    for i in range(size_n - 1, -1, -1):
        value = values[i]
        for j in range(i + 1, size_n):
            value = value - entries[i][j] * result[j]
        result[i] = value / entries[i][i]
    return result


def columns_at(iteration):
    return list(range(max(1, iteration - MEM + 1), iteration + 1))


def on_device(
    network,
    upper_bound,
    build_cost,
    unit_cost,
    demand,
    inflow,
    primal_start,
    network_start,
    energy_start,
    build_start,
    accepted,
    restarts,
):
    tm_count, bus_count = lax.axis_size("tm"), lax.axis_size("bus")
    tm, bus = lax.axis_index("tm"), lax.axis_index("bus")
    hours, width = primal_start.shape
    blocks = lane_blocks(width)
    flags = jnp.concatenate([accepted, restarts, tm.astype(jnp.int32).reshape(1)])
    first_restart, place_tm = accepted.shape[0], 2 * accepted.shape[0]
    member = shape(hours, width)
    line = shape(1, width)
    row = shape(1, LANES)
    tile = shape(ROWS, LANES)
    kind = {X: member, Y: member, E: member, U: line, SLOPE: member, COLUMN: line}

    upper_bound, build_cost, inflow, build_start = (
        value.reshape(1, width) for value in (upper_bound, build_cost, inflow, build_start)
    )
    own_high, own_low, other_high, other_low = split_network(
        network, bus.astype(jnp.int32).reshape(1)
    )


    def swap(value):
        return lax.ppermute(value, "bus", [(i, (i + 1) % bus_count) for i in range(bus_count)])

    def partner(value, distance):
        return lax.ppermute(value, "tm", [(i, i ^ distance) for i in range(tm_count)])

    def distances():
        return [1 << i for i in range(tm_count.bit_length() - 1)]

    def sums_of(value, backward, parts):
        beyond = jnp.zeros((1, parts), f32)
        for distance in distances():
            arrived = partner(value, distance)
            mine = (tm & distance) == 0
            take = mine if backward else ~mine
            beyond = beyond + jnp.where(take, arrived[:, :parts], 0.0)
            value = value + arrived
        return value, beyond


    def restart_of(ref, iteration):
        return ref[first_restart + iteration - 1].astype(f32)

    def counter_of(ref, iteration):
        count = jnp.float32(1.0)
        for k in range(1, iteration):
            count = (1.0 - restart_of(ref, k)) * count + 1.0
        return count

    def active_of(ref, column, iteration):
        value = jnp.float32(1.0)
        for k in range(column, iteration + 1):
            value = value * (1.0 - restart_of(ref, k))
        return value

    def weight_of(ref):
        at = ref[place_tm] * hours + row_iota(hours) + 1
        return 1.0 / at.astype(f32)

    def on_diagonal():
        lane = lax.broadcasted_iota(jnp.int32, (ROWS, LANES), 1)
        return lane == row_iota(ROWS)

    def mixing(i, iteration, products, log):
        columns = columns_at(iteration)
        size_n = len(columns)
        spread = jnp.where(on_diagonal(), jnp.broadcast_to(products, (ROWS, LANES)), 0.0)
        newest = jnp.broadcast_to(jnp.sum(spread, axis=1, keepdims=True), (ROWS, LANES))
        summed = dict(zip(columns[:-1], [ref[...] for ref in i.log]))
        summed[iteration] = newest
        log[...] = newest
        active = [active_of(i.flags, k, iteration) for k in columns]

        def entry(a, b):
            a, b = max(a, b), min(a, b)
            at = columns_at(columns[a]).index(columns[b])
            return summed[columns[a]][at : at + 1]

        gram = [[entry(a, b) for b in range(size_n)] for a in range(size_n)]
        trace = gram[0][0] * active[0]
        for a in range(1, size_n):
            trace = trace + gram[a][a] * active[a]
        shift = 0.001 * trace / size_n + 1e-06
        system = [
            [gram[a][b] * (active[a] * active[b]) for b in range(size_n)] for a in range(size_n)
        ]
        for a in range(size_n):
            system[a][a] = system[a][a] + (1.0 - active[a]) + shift
        right = [newest[8 + a : 9 + a] * active[a] for a in range(size_n)]
        mix = solve_rows(system, right)
        accept = i.flags[iteration - 1].astype(f32)
        return [accept * (value * a) for value, a in zip(mix, active)]

    def mixed(mapped, deltas, coefs):
        if not coefs:
            return mapped
        correction = coefs[0] * deltas[0]
        for coef, delta in zip(coefs[1:], deltas[1:]):
            correction = correction + coef * delta
        return mapped - correction

    def restarted(ref, iteration, following, total):
        if iteration == 0:
            return following, None
        restart = restart_of(ref, iteration)
        total = following if total is None else total + following
        mean = total / counter_of(ref, iteration)
        return jnp.where(restart > 0.5, mean, following), (1.0 - restart) * total

    def begin(i, o, k, at, name, mapped, deltas, coefs):
        following = mixed(mapped, deltas, coefs)
        total = i.totals[name][at] if k >= 2 else None
        state, total = restarted(i.flags, k, following, total)
        if k >= 1:
            o.totals[name][at] = total
        return state

    def note(i, o, k, at, name, mapped, state, pairs):
        residual = mapped - state
        o.resid[name][at] = residual
        if k == 0:
            return
        o.delta[name][at] = mapped - i.last_map[name][at]
        newest = residual - i.resid[name][at]
        o.column[name][at] = newest
        for j, column in enumerate([ref[at] for ref in i.columns[name]] + [newest]):
            for index, other in ((j, newest), (8 + j, residual)):
                term = column * other
                if name != U:
                    term = to_tile(term)
                key = (name == U, index)
                pairs[key] = pairs[key] + term if key in pairs else term

    def pair_tile(pairs, scale=1.0):
        rows = []
        for index in range(ROWS):
            total = jnp.zeros((1, LANES), f32)
            if (False, index) in pairs:
                total = jnp.sum(pairs[False, index], axis=0, keepdims=True)
            if (True, index) in pairs:
                total = total + scale * pairs[True, index]
            rows.append(total)
        return jnp.concatenate(rows, axis=0)


    def first_kernel(i, o):
        weight_at = weight_of(i.flags)
        for sl in blocks:
            tail = tail_sum(i.energy[:, sl] * weight_at)
            o.tail[:, sl] = tail
            o.message[:, sl] = tail[0:1]
        o.message[:, width:] = jnp.zeros((1, LANES), f32)

    def primal_kernel(k):
        count = len(columns_at(k - 1)) if k >= 2 else 0

        def primal(i, o):
            coefs = mixing(i, k - 1, i.message[:, width:], o.log) if k >= 2 else []
            for j, coef in enumerate(coefs):
                o.coefs[j : j + 1, :] = coef
            for sl in blocks:
                at = (slice(None), sl)
                slope = (i.pulled_own[at] + i.pulled_other[at]) - (i.tail[at] + i.later[at])
                column = i.message[at]
                state = {}
                for name, mapped in ((SLOPE, slope), (COLUMN, column)):
                    o.mapped[name][at] = mapped
                    deltas = [ref[at] for ref in i.deltas[name]] if count else []
                    if count:
                        newest = mapped - i.last_map[name][at]
                        o.delta[name][at] = newest
                        deltas.append(newest)
                    state[name] = begin(i, o, k, at, name, mapped, deltas, coefs)
                for name in (X, U):
                    deltas = [ref[at] for ref in i.deltas[name]] if count else []
                    state[name] = begin(i, o, k, at, name, i.mapped[name][at], deltas, coefs)
                    o.state[name][at] = state[name]
                next_primal = jnp.clip(
                    state[X] - primal_step * (i.unit_cost[at] - state[SLOPE]),
                    0.0,
                    i.upper_bound[at],
                )
                next_build = jnp.maximum(
                    state[U] - primal_step * (i.build_cost[at] - state[COLUMN]), 0.0
                )
                bar = 2.0 * next_primal - state[X]
                o.mapped[X][at] = next_primal
                o.mapped[U][at] = next_build
                o.bar[at] = bar
                o.block[at] = jnp.sum(bar, axis=0, keepdims=True)

        return primal

    def push_kernel(k):
        count = len(columns_at(k - 1)) if k >= 2 else 0

        def push(i, o):
            o.pushed[...] = product(i.bar[...], i.high[...], i.low[...], True)
            coefs = [i.coefs[j : j + 1, :] for j in range(count)]
            pairs = {}
            for sl in blocks:
                at = (slice(None), sl)
                for name in (Y, E):
                    deltas = [ref[at] for ref in i.deltas[name]] if count else []
                    o.state[name][at] = begin(
                        i, o, k, at, name, i.mapped[name][at], deltas, coefs
                    )
                o.running[at] = running_sum(i.bar[at])
                note(i, o, k, at, X, i.next_primal[at], i.primal[at], pairs)
            o.pairs[...] = pair_tile(pairs)

        return push

    def dual_kernel(k):
        def dual(i, o):
            o.mapped[...] = i.pushed[...] + product(
                i.bar_other[...], i.high[...], i.low[...], True
            )
            pairs = {}
            for sl in blocks:
                at = (slice(None), sl)
                state = i.state[at]
                mapped = jnp.maximum(state + dual_step * (i.demand[at] - o.mapped[at]), 0.0)
                o.mapped[at] = mapped
                note(i, o, k, at, Y, mapped, state, pairs)
            o.pairs[...] = i.pairs[...] + pair_tile(pairs)

        return dual

    def energy_kernel(k):
        def energy(i, o):
            weight_at = weight_of(i.flags)
            own_build = (i.flags[place_tm] == 0).astype(f32)
            pairs = {}
            for sl in blocks:
                at = (slice(None), sl)
                running = i.running[at] + i.earlier[at]
                state, build, next_build = i.state[E][at], i.state[U][at], i.mapped[at]
                bar_build = 2.0 * next_build - build
                mapped = jnp.maximum(
                    state + dual_step * (-i.inflow[at] - (bar_build - running) * weight_at), 0.0
                )
                o.mapped[at] = mapped
                tail = tail_sum(mapped * weight_at)
                o.tail[at] = tail
                o.block[at] = tail[0:1]
                note(i, o, k, at, E, mapped, state, pairs)
                note(i, o, k, at, U, next_build, build, pairs)
            if k >= 1:
                lines = i.pairs[...] + pair_tile(pairs, own_build)
                sums = jnp.broadcast_to(jnp.sum(lines, axis=1, keepdims=True), (ROWS, LANES))
                o.products[...] = jnp.sum(
                    jnp.where(on_diagonal(), sums, 0.0), axis=0, keepdims=True
                )
            else:
                o.products[...] = jnp.zeros((1, LANES), f32)

        return energy

    def pull_kernel(i, o):
        o.pulled[...] = product(i.dual[...], i.high[...], i.low[...], False)

    def last_kernel(i, o):
        coefs = mixing(i, ITERS - 1, i.message[...], o.log)
        for name in (X, Y, E, U):
            for sl in blocks:
                at = (slice(None), sl)
                deltas = [ref[at] for ref in i.deltas[name]]
                o.following[name][at] = mixed(i.mapped[name][at], deltas, coefs)


    mapped = {X: primal_start, Y: network_start, E: energy_start, U: build_start}
    deltas = {name: [] for name in kind}
    columns = {name: [] for name in (X, Y, E, U)}
    totals, last_map, resid, logs = {}, {}, {}, {}

    def pull(dual):
        out = run(pull_kernel, dict(dual=dual, high=other_high, low=other_low), dict(pulled=member))
        arriving = swap(out.pulled)
        out = run(pull_kernel, dict(dual=dual, high=own_high, low=own_low), dict(pulled=member))
        return out.pulled, arriving

    def picked(source, names):
        return {name: source[name] for name in names}

    def kinds(*names):
        return picked(kind, names)

    def note_ins(k, names):
        if k == 0:
            return {}
        return dict(
            last_map=picked(last_map, names),
            resid=picked(resid, names),
            columns={name: columns[name][-(MEM - 1) :] for name in names},
        )

    def note_outs(k, names):
        each = kinds(*names)
        return dict(resid=each, **(dict(delta=each, column=each) if k else {}))

    def take(k, out, names):
        for name in names:
            resid[name] = out.resid[name]
            if k:
                deltas[name] = (deltas[name] + [out.delta[name]])[-MEM:]
                columns[name] = (columns[name] + [out.column[name]])[-MEM:]

    def log_ins(iteration):
        return [logs[j] for j in columns_at(iteration)[:-1]]

    out = run(
        first_kernel,
        dict(flags=flags, energy=energy_start),
        dict(tail=member, message=shape(1, width + LANES)),
    )
    tail = out.tail
    message, later = sums_of(out.message, True, width)
    pulled_own, pulled_other = pull(network_start)

    for k in range(ITERS):
        mixes = k >= 2
        ins = dict(
            flags=flags,
            message=message,
            later=later,
            pulled_own=pulled_own,
            pulled_other=pulled_other,
            tail=tail,
            mapped=picked(mapped, (X, U)),
            unit_cost=unit_cost,
            upper_bound=upper_bound,
            build_cost=build_cost,
        )
        outs = dict(
            mapped=kinds(SLOPE, COLUMN, X, U),
            state=kinds(X, U),
            bar=member,
            block=line,
        )
        if mixes:
            ins.update(
                log=log_ins(k - 1),
                last_map=picked(last_map, (SLOPE, COLUMN)),
                totals=picked(totals, (SLOPE, COLUMN, X, U)),
                deltas={
                    SLOPE: deltas[SLOPE][-(MEM - 1) :],
                    COLUMN: deltas[COLUMN][-(MEM - 1) :],
                    X: deltas[X],
                    U: deltas[U],
                },
            )
            outs.update(log=tile, coefs=shape(8, LANES), delta=kinds(SLOPE, COLUMN))
        if k >= 1:
            outs.update(totals=kinds(SLOPE, COLUMN, X, U))
        one = run(primal_kernel(k), ins, outs)
        if mixes:
            logs[k - 1] = one.log
            for name in (SLOPE, COLUMN):
                deltas[name] = (deltas[name] + [one.delta[name]])[-MEM:]
        for name in (SLOPE, COLUMN):
            last_map[name] = one.mapped[name]
        if k >= 1:
            totals.update(one.totals)
        _, earlier = sums_of(one.block, False, width)
        bar_other = swap(one.bar)

        ins = dict(
            flags=flags,
            bar=one.bar,
            next_primal=one.mapped[X],
            primal=one.state[X],
            mapped=picked(mapped, (Y, E)),
            high=own_high,
            low=own_low,
            **note_ins(k, (X,)),
        )
        outs = dict(
            pushed=member,
            state=kinds(Y, E),
            running=member,
            pairs=tile,
            **note_outs(k, (X,)),
        )
        if mixes:
            ins.update(
                coefs=one.coefs, deltas=picked(deltas, (Y, E)), totals=picked(totals, (Y, E))
            )
        if k >= 1:
            outs.update(totals=kinds(Y, E))
        two = run(push_kernel(k), ins, outs)
        if k >= 1:
            totals.update(two.totals)

        three = run(
            dual_kernel(k),
            dict(
                pushed=two.pushed,
                bar_other=bar_other,
                state=two.state[Y],
                demand=demand,
                pairs=two.pairs,
                high=other_high,
                low=other_low,
                **note_ins(k, (Y,)),
            ),
            dict(mapped=member, pairs=tile, **note_outs(k, (Y,))),
        )
        four = run(
            energy_kernel(k),
            dict(
                flags=flags,
                running=two.running,
                earlier=earlier,
                state={E: two.state[E], U: one.state[U]},
                mapped=one.mapped[U],
                inflow=inflow,
                pairs=three.pairs,
                **note_ins(k, (E, U)),
            ),
            dict(mapped=member, tail=member, block=line, products=row, **note_outs(k, (E, U))),
        )
        take(k, two, (X,))
        take(k, three, (Y,))
        take(k, four, (E, U))
        mapped = {X: one.mapped[X], Y: three.mapped, E: four.mapped, U: one.mapped[U]}
        last_map.update(mapped)
        tail = four.tail
        products = four.products + swap(four.products) if k else four.products
        if k < ITERS - 1:
            message, later = sums_of(
                jnp.concatenate([four.block, products], axis=1), True, width
            )
            pulled_own, pulled_other = pull(mapped[Y])
        else:
            message, _ = sums_of(products, True, LANES)

    out = run(
        last_kernel,
        dict(
            flags=flags,
            message=message,
            log=log_ins(ITERS - 1),
            mapped=mapped,
            deltas=picked(deltas, (X, Y, E, U)),
        ),
        dict(log=tile, following=kinds(X, Y, E, U)),
    )
    final = out.following
    return final[X], final[Y], final[E], final[U].reshape(width)


def solution(mesh):
    hourly = P(("grp", "tm"), "bus")
    return jax.shard_map(
        on_device,
        mesh=mesh,
        in_specs=(
            P("bus", None),
            P("bus"),
            P("bus"),
            hourly,
            hourly,
            P(("grp", "bus")),
            hourly,
            hourly,
            hourly,
            P(("grp", "bus")),
            P("grp"),
            P("grp"),
        ),
        out_specs=(hourly, hourly, hourly, P(("grp", "bus"))),
        check_vma=False,
    )
```

time: 1970 us -> 299 us (0.15); the launches traced: 1950 us -> 295 us
  blocking collectives: 967 us -> 0 us
  between operations: 362 us -> 1.52 us
  other arithmetic: 316 us -> 1.36 us
  matrix products: 184 us -> 0 us
  waiting for transfers between devices: 0.22 us -> 107 us
  starting transfers between devices: 0.37 us -> 102 us
  local copies, waits for them, and re-layouts: 113 us -> 13.3 us
  Pallas kernels: 0 us -> 69.5 us
    all_gather x27 -> x0, blocking collectives: 570 us -> none  [the longest x18 551 us: carried_in(): pieces = lax.all_gather(value, axis)]
    psum x17 -> x0, blocking collectives: 397 us -> none  [the longest x8 237 us: on_device(): summed_row, summed_right = lax.psum((local_row, local_right), ('tm', 'bus'))]
    dot_general x36 -> x0, matrix products: 184 us -> none  [the longest x9 104 us: advance(): lax.dot_general(lax.all_gather(bar_primal, 'bus', axis=1, tiled=True), ne...]
    ppermute x0 -> x83, waiting for transfers between devices: none -> 107 us  [the longest x57 96.9 us: partner(): lax.ppermute(value, 'tm', [(i, i ^ distance) for i in range(tm_count)])]
    ppermute x0 -> x83, starting transfers between devices: none -> 102 us  [the longest x57 101 us: partner(): lax.ppermute(value, 'tm', [(i, i ^ distance) for i in range(tm_count)])]
    select_n x126 -> x0, other arithmetic: 83.9 us -> none  [step(): return jnp.where(position < mine, longer, subtotal)]
    sub x37 -> x0, other arithmetic: 83.5 us -> none  [the longest x9 35.7 us: on_device(): following.append(mapped[b] - accept_flag * correction)]
    pallas_call x0 -> x57, Pallas kernels: none -> 69.5 us  [the longest x56 67.2 us: run(): pl.pallas_call(kernel, out_shape=out_leaves, in_specs=[place(leaf) for le...]
  transfers between devices with their start and end apart: 9 -> 83, of which waited for: 0 -> 64; matrix products, arithmetic and copies ran while one was open for 5% -> 0% of each run, Pallas kernels for 0% -> 12%
where the time goes in v1:
time: 299 us; the launch traced here: 295 us
  waiting for transfers between devices  107 us (36%)
  starting transfers between devices  102 us (34%)
  Pallas kernels  69.5 us (23%)
  local copies, waits for them, and re-layouts  13.3 us (4%)
    ppermute x57, starting transfers between devices, partner(): lax.ppermute(value, 'tm', [(i, i ^ distance) for i in range(tm_count)])  101 us
    ppermute x57, waiting for transfers between devices, partner(): lax.ppermute(value, 'tm', [(i, i ^ distance) for i in range(tm_count)])  96.9 us
    pallas_call x56, Pallas kernels, run(): pl.pallas_call(kernel, out_shape=out_leaves, in_specs=[place(leaf) for le...  67.2 us
    unnamed x43, local copies, waits for them, and re-layouts  13.2 us
    ppermute x26, waiting for transfers between devices, swap(): lax.ppermute(value, 'bus', [(i, (i + 1) % bus_count) for i in range(bus_c...  10.4 us
  transfers between devices with their start and end apart: 83, of which 64 were waited for; matrix products, arithmetic and copies ran while one was open for 0% of the time, Pallas kernels for 12%

profile of v1, /device:TPU:0, one launch (start us, length us, event | category | flops | bytes accessed | tf_op | source)
XLA Modules:
  0.0 295.0 jit_solution(9208691376406728555)
XLA Ops:
  2.9 3.0 %collective-permute-start = (f32[1,1152]{1,0:T(1,128)S(1)}, f32[1,1152]{1,0:T(1,128)S(1)}, u32[]{:S(2)}, u32[]{:S(2)}) collective-permute-start(f32[1,1152]{1,0:T(1,128)S(1)} %get-tuple-element.339), channel_id=1, source_target_pairs={{0,2},{2,0},{4,6},{6,4},{8,10},{10,8},{12,14},{14,12},{1,3},{3,1},... | collective-permute-start | bytes 13832 | tf_op jit(solution)/shard_map/ppermute | solution.py:188
  5.9 1.6 collective-permute-done
  7.5 2.1 collective-permute-start.1
  11.2 3.0 %collective-permute-start.2 = (f32[1,1152]{1,0:T(1,128)S(1)}, f32[1,1152]{1,0:T(1,128)S(1)}, u32[]{:S(2)}, u32[]{:S(2)}) collective-permute-start(f32[1,1152]{1,0:T(1,128)S(1)} %add.278), channel_id=1, source_target_pairs={{0,8},{2,10},{4,12},{6,14},{8,0},{10,2},{12,4},{14,6},{1,9},{3,11}... | collective-permute-start | bytes 13832 | tf_op jit(solution)/shard_map/ppermute | solution.py:188
  14.2 3.4 %copy-done.10 = f32[1024,2048]{1,0:T(8,128)S(1)} copy-done((f32[1024,2048]{1,0:T(8,128)S(1)}, f32[1024,2048]{1,0:T(8,128)}, u32[]{:S(2)}) %copy-start.10) | copy-done | bytes 8388632
  17.6 2.3 shard_map.147
  30.2 2.1 collective-permute-done.4
  33.9 2.0 collective-permute-done.5
  39.2 1.9 push.9
  43.3 1.8 collective-permute-start.8
  45.1 1.9 collective-permute-done.8
  46.9 1.8 collective-permute-start.9
  48.7 1.8 collective-permute-done.9
  50.6 2.8 collective-permute-start.10
  58.6 2.1 collective-permute-done.12
  62.3 2.0 collective-permute-done.13
  65.9 1.9 push.10
  73.8 2.1 collective-permute-done.17
  75.9 1.6 collective-permute-start.18
  77.5 2.0 collective-permute-done.18
  86.5 2.1 collective-permute-done.21
  90.2 2.0 collective-permute-done.22
  93.8 2.0 push.11
  101.7 2.1 collective-permute-done.26
  103.8 1.6 collective-permute-start.27
  105.5 2.0 collective-permute-done.27
  114.7 2.1 collective-permute-done.30
  118.4 2.0 collective-permute-done.31
  121.8 2.1 push.12
  129.9 2.1 collective-permute-done.35
  132.1 1.6 collective-permute-start.36
  133.7 2.0 collective-permute-done.36
  142.8 2.1 collective-permute-done.39
  146.5 2.0 collective-permute-done.40
  149.9 2.1 push.13
  158.1 2.1 collective-permute-done.44
  160.2 1.6 collective-permute-start.45
  161.8 2.0 collective-permute-done.45
  171.0 2.1 collective-permute-done.48
  174.7 2.0 collective-permute-done.49
  178.1 2.1 push.14
  186.4 2.1 collective-permute-done.53
  188.5 11.7 %collective-permute-start.54 = (f32[1,1152]{1,0:T(1,128)S(1)}, f32[1,1152]{1,0:T(1,128)S(1)}, u32[]{:S(2)}, u32[]{:S(2)}) collective-permute-start(f32[1,1152]{1,0:T(1,128)S(1)} %fusion.38), channel_id=1, source_target_pairs={{0,4},{2,6},{4,0},{6,2},{8,12},{10,14},{12,8},{14,10},{1,5},{3,7},... | collective-permute-start | bytes 13832 | tf_op jit(solution)/shard_map/ppermute | solution.py:188
  200.2 2.0 collective-permute-done.54
  209.4 2.1 collective-permute-done.57
  213.1 2.0 collective-permute-done.58
  216.5 2.2 push.15
  224.8 2.1 collective-permute-done.62
  226.9 1.6 collective-permute-start.63
  228.5 2.0 collective-permute-done.63
  237.8 2.1 collective-permute-done.66
  241.4 2.0 collective-permute-done.67
  244.9 2.2 push.16
  253.1 2.1 collective-permute-done.71
  255.2 1.6 collective-permute-start.72
  256.9 2.0 collective-permute-done.72
  263.4 1.8 primal.17
  266.8 2.1 collective-permute-done.76
  270.5 2.0 collective-permute-done.77
  273.9 2.8 push.17
  277.0 2.1 dual.17
  283.3 2.0 collective-permute-done.80
  286.9 2.0 collective-permute-done.81
  290.2 3.1 %collective-permute-done.82 = f32[1,128]{1,0:T(1,128)S(1)} collective-permute-done((f32[1,128]{1,0:T(1,128)S(1)}, f32[1,128]{1,0:T(1,128)S(1)}, u32[]{:S(2)}, u32[]{:S(2)}) %collective-permute-start.82) | collective-permute-done | bytes 544 | tf_op jit(solution)/shard_map/ppermute | solution.py:188
  (285 shorter events, 150.3 us)
Async XLA Ops:
  2.9 4.6 %collective-permute-start = (f32[1,1152]{1,0:T(1,128)S(1)}, f32[1,1152]{1,0:T(1,128)S(1)}, u32[]{:S(2)}, u32[]{:S(2)}) collective-permute-start(f32[1,1152]{1,0:T(1,128)S(1)} %get-tuple-element.339), channel_id=1, source_target_pairs={{0,2},{2,0},{4,6},{6,4},{8,10},{10,8},{12,14},{14,12},{1,3},{3,1},... | collective-permute-start | bytes 13832 | tf_op jit(solution)/shard_map/ppermute | solution.py:188
  7.5 3.7 %collective-permute-start.1 = (f32[1,1152]{1,0:T(1,128)S(1)}, f32[1,1152]{1,0:T(1,128)S(1)}, u32[]{:S(2)}, u32[]{:S(2)}) collective-permute-start(f32[1,1152]{1,0:T(1,128)S(1)} %add.276), channel_id=1, source_target_pairs={{0,4},{2,6},{4,0},{6,2},{8,12},{10,14},{12,8},{14,10},{1,5},{3,7},... | collective-permute-start | bytes 13832 | tf_op jit(solution)/shard_map/ppermute | solution.py:188
  11.2 16.1 %collective-permute-start.2 = (f32[1,1152]{1,0:T(1,128)S(1)}, f32[1,1152]{1,0:T(1,128)S(1)}, u32[]{:S(2)}, u32[]{:S(2)}) collective-permute-start(f32[1,1152]{1,0:T(1,128)S(1)} %add.278), channel_id=1, source_target_pairs={{0,8},{2,10},{4,12},{6,14},{8,0},{10,2},{12,4},{14,6},{1,9},{3,11}... | collective-permute-start | bytes 13832 | tf_op jit(solution)/shard_map/ppermute | solution.py:188
  23.2 4.1 %collective-permute-start.3 = (f32[32,1024]{1,0:T(8,128)S(1)}, f32[32,1024]{1,0:T(8,128)S(1)}, u32[]{:S(2)}, u32[]{:S(2)}) collective-permute-start(f32[32,1024]{1,0:T(8,128)S(1)} %pull_kernel.18), channel_id=1, source_target_pairs={{0,1},{1,0},{2,3},{3,2},{4,5},{5,4},{6,7},{7,6},{8,9},{9,8},{10,11... | collective-permute-start | bytes 393224 | tf_op jit(solution)/shard_map/ppermute | solution.py:185
  28.7 3.6 %collective-permute-start.4 = (f32[1,1024]{1,0:T(1,128)S(1)}, f32[1,1024]{1,0:T(1,128)S(1)}, u32[]{:S(2)}, u32[]{:S(2)}) collective-permute-start(f32[1,1024]{1,0:T(1,128)S(1)} %get-tuple-element.345), channel_id=1, source_target_pairs={{0,2},{2,0},{4,6},{6,4},{8,10},{10,8},{12,14},{14,12},{1,3},{3,1},... | collective-permute-start | bytes 12296 | tf_op jit(solution)/shard_map/ppermute | solution.py:188
  32.3 3.6 %collective-permute-start.5 = (f32[1,1024]{1,0:T(1,128)S(1)}, f32[1,1024]{1,0:T(1,128)S(1)}, u32[]{:S(2)}, u32[]{:S(2)}) collective-permute-start(f32[1,1024]{1,0:T(1,128)S(1)} %add.281), channel_id=1, source_target_pairs={{0,4},{2,6},{4,0},{6,2},{8,12},{10,14},{12,8},{14,10},{1,5},{3,7},... | collective-permute-start | bytes 12296 | tf_op jit(solution)/shard_map/ppermute | solution.py:188
  35.9 5.2 %collective-permute-start.6 = (f32[1,1024]{1,0:T(1,128)S(1)}, f32[1,1024]{1,0:T(1,128)S(1)}, u32[]{:S(2)}, u32[]{:S(2)}) collective-permute-start(f32[1,1024]{1,0:T(1,128)S(1)} %add.283), channel_id=1, source_target_pairs={{0,8},{2,10},{4,12},{6,14},{8,0},{10,2},{12,4},{14,6},{1,9},{3,11}... | collective-permute-start | bytes 12296 | tf_op jit(solution)/shard_map/ppermute | solution.py:188
  35.9 5.2 %collective-permute-start.7 = (f32[32,1024]{1,0:T(8,128)S(1)}, f32[32,1024]{1,0:T(8,128)S(1)}, u32[]{:S(2)}, u32[]{:S(2)}) collective-permute-start(f32[32,1024]{1,0:T(8,128)S(1)} %get-tuple-element.347.refs_0_), channel_id=1, source_target_pairs={{0,1},{1,0},{2,3},{3,2},{4,5},{5,4},{6,7},{7,6},{8,9},{9,8},{10,11... | collective-permute-start | bytes 393224 | tf_op jit(solution)/shard_map/ppermute | solution.py:185
  43.3 3.7 %collective-permute-start.8 = (f32[1,1152]{1,0:T(1,128)S(1)}, f32[1,1152]{1,0:T(1,128)S(1)}, u32[]{:S(2)}, u32[]{:S(2)}) collective-permute-start(f32[1,1152]{1,0:T(1,128)S(1)} %constant_dynamic-update-slice_fusion), channel_id=1, source_target_pairs={{0,2},{2,0},{4,6},{6,4},{8,10},{10,8},{12,14},{14,12},{1,3},{3,1},... | collective-permute-start | bytes 13832 | tf_op jit(solution)/shard_map/ppermute | solution.py:188
  46.9 3.6 %collective-permute-start.9 = (f32[1,1152]{1,0:T(1,128)S(1)}, f32[1,1152]{1,0:T(1,128)S(1)}, u32[]{:S(2)}, u32[]{:S(2)}) collective-permute-start(f32[1,1152]{1,0:T(1,128)S(1)} %add.285), channel_id=1, source_target_pairs={{0,4},{2,6},{4,0},{6,2},{8,12},{10,14},{12,8},{14,10},{1,5},{3,7},... | collective-permute-start | bytes 13832 | tf_op jit(solution)/shard_map/ppermute | solution.py:188
  50.6 4.5 %collective-permute-start.10 = (f32[1,1152]{1,0:T(1,128)S(1)}, f32[1,1152]{1,0:T(1,128)S(1)}, u32[]{:S(2)}, u32[]{:S(2)}) collective-permute-start(f32[1,1152]{1,0:T(1,128)S(1)} %add.287), channel_id=1, source_target_pairs={{0,8},{2,10},{4,12},{6,14},{8,0},{10,2},{12,4},{14,6},{1,9},{3,11}... | collective-permute-start | bytes 13832 | tf_op jit(solution)/shard_map/ppermute | solution.py:188
  57.0 3.7 %collective-permute-start.12 = (f32[1,1024]{1,0:T(1,128)S(1)}, f32[1,1024]{1,0:T(1,128)S(1)}, u32[]{:S(2)}, u32[]{:S(2)}) collective-permute-start(f32[1,1024]{1,0:T(1,128)S(1)} %get-tuple-element.367), channel_id=1, source_target_pairs={{0,2},{2,0},{4,6},{6,4},{8,10},{10,8},{12,14},{14,12},{1,3},{3,1},... | collective-permute-start | bytes 12296 | tf_op jit(solution)/shard_map/ppermute | solution.py:188
  60.7 3.6 %collective-permute-start.13 = (f32[1,1024]{1,0:T(1,128)S(1)}, f32[1,1024]{1,0:T(1,128)S(1)}, u32[]{:S(2)}, u32[]{:S(2)}) collective-permute-start(f32[1,1024]{1,0:T(1,128)S(1)} %add.290), channel_id=1, source_target_pairs={{0,4},{2,6},{4,0},{6,2},{8,12},{10,14},{12,8},{14,10},{1,5},{3,7},... | collective-permute-start | bytes 12296 | tf_op jit(solution)/shard_map/ppermute | solution.py:188
  64.3 4.5 %collective-permute-start.14 = (f32[1,1024]{1,0:T(1,128)S(1)}, f32[1,1024]{1,0:T(1,128)S(1)}, u32[]{:S(2)}, u32[]{:S(2)}) collective-permute-start(f32[1,1024]{1,0:T(1,128)S(1)} %add.292), channel_id=1, source_target_pairs={{0,8},{2,10},{4,12},{6,14},{8,0},{10,2},{12,4},{14,6},{1,9},{3,11}... | collective-permute-start | bytes 12296 | tf_op jit(solution)/shard_map/ppermute | solution.py:188
  72.2 3.7 %collective-permute-start.17 = (f32[1,1152]{1,0:T(1,128)S(1)}, f32[1,1152]{1,0:T(1,128)S(1)}, u32[]{:S(2)}, u32[]{:S(2)}) collective-permute-start(f32[1,1152]{1,0:T(1,128)S(1)} %pad_maximum_fusion), channel_id=1, source_target_pairs={{0,2},{2,0},{4,6},{6,4},{8,10},{10,8},{12,14},{14,12},{1,3},{3,1},... | collective-permute-start | bytes 13832 | tf_op jit(solution)/shard_map/ppermute | solution.py:188
  75.9 3.7 %collective-permute-start.18 = (f32[1,1152]{1,0:T(1,128)S(1)}, f32[1,1152]{1,0:T(1,128)S(1)}, u32[]{:S(2)}, u32[]{:S(2)}) collective-permute-start(f32[1,1152]{1,0:T(1,128)S(1)} %fusion.42), channel_id=1, source_target_pairs={{0,4},{2,6},{4,0},{6,2},{8,12},{10,14},{12,8},{14,10},{1,5},{3,7},... | collective-permute-start | bytes 13832 | tf_op jit(solution)/shard_map/ppermute | solution.py:188
  79.6 4.5 %collective-permute-start.19 = (f32[1,1152]{1,0:T(1,128)S(1)}, f32[1,1152]{1,0:T(1,128)S(1)}, u32[]{:S(2)}, u32[]{:S(2)}) collective-permute-start(f32[1,1152]{1,0:T(1,128)S(1)} %add.297), channel_id=1, source_target_pairs={{0,8},{2,10},{4,12},{6,14},{8,0},{10,2},{12,4},{14,6},{1,9},{3,11}... | collective-permute-start | bytes 13832 | tf_op jit(solution)/shard_map/ppermute | solution.py:188
  84.9 3.7 %collective-permute-start.21 = (f32[1,1024]{1,0:T(1,128)S(1)}, f32[1,1024]{1,0:T(1,128)S(1)}, u32[]{:S(2)}, u32[]{:S(2)}) collective-permute-start(f32[1,1024]{1,0:T(1,128)S(1)} %get-tuple-element.404), channel_id=1, source_target_pairs={{0,2},{2,0},{4,6},{6,4},{8,10},{10,8},{12,14},{14,12},{1,3},{3,1},... | collective-permute-start | bytes 12296 | tf_op jit(solution)/shard_map/ppermute | solution.py:188
  88.6 3.6 %collective-permute-start.22 = (f32[1,1024]{1,0:T(1,128)S(1)}, f32[1,1024]{1,0:T(1,128)S(1)}, u32[]{:S(2)}, u32[]{:S(2)}) collective-permute-start(f32[1,1024]{1,0:T(1,128)S(1)} %add.300), channel_id=1, source_target_pairs={{0,4},{2,6},{4,0},{6,2},{8,12},{10,14},{12,8},{14,10},{1,5},{3,7},... | collective-permute-start | bytes 12296 | tf_op jit(solution)/shard_map/ppermute | solution.py:188
  92.2 4.5 %collective-permute-start.23 = (f32[1,1024]{1,0:T(1,128)S(1)}, f32[1,1024]{1,0:T(1,128)S(1)}, u32[]{:S(2)}, u32[]{:S(2)}) collective-permute-start(f32[1,1024]{1,0:T(1,128)S(1)} %add.302), channel_id=1, source_target_pairs={{0,8},{2,10},{4,12},{6,14},{8,0},{10,2},{12,4},{14,6},{1,9},{3,11}... | collective-permute-start | bytes 12296 | tf_op jit(solution)/shard_map/ppermute | solution.py:188
  100.1 3.7 %collective-permute-start.26 = (f32[1,1152]{1,0:T(1,128)S(1)}, f32[1,1152]{1,0:T(1,128)S(1)}, u32[]{:S(2)}, u32[]{:S(2)}) collective-permute-start(f32[1,1152]{1,0:T(1,128)S(1)} %pad_maximum_fusion.1), channel_id=1, source_target_pairs={{0,2},{2,0},{4,6},{6,4},{8,10},{10,8},{12,14},{14,12},{1,3},{3,1},... | collective-permute-start | bytes 13832 | tf_op jit(solution)/shard_map/ppermute | solution.py:188
  103.8 3.7 %collective-permute-start.27 = (f32[1,1152]{1,0:T(1,128)S(1)}, f32[1,1152]{1,0:T(1,128)S(1)}, u32[]{:S(2)}, u32[]{:S(2)}) collective-permute-start(f32[1,1152]{1,0:T(1,128)S(1)} %fusion.41), channel_id=1, source_target_pairs={{0,4},{2,6},{4,0},{6,2},{8,12},{10,14},{12,8},{14,10},{1,5},{3,7},... | collective-permute-start | bytes 13832 | tf_op jit(solution)/shard_map/ppermute | solution.py:188
  107.5 4.5 %collective-permute-start.28 = (f32[1,1152]{1,0:T(1,128)S(1)}, f32[1,1152]{1,0:T(1,128)S(1)}, u32[]{:S(2)}, u32[]{:S(2)}) collective-permute-start(f32[1,1152]{1,0:T(1,128)S(1)} %add.307), channel_id=1, source_target_pairs={{0,8},{2,10},{4,12},{6,14},{8,0},{10,2},{12,4},{14,6},{1,9},{3,11}... | collective-permute-start | bytes 13832 | tf_op jit(solution)/shard_map/ppermute | solution.py:188
  113.1 3.7 %collective-permute-start.30 = (f32[1,1024]{1,0:T(1,128)S(1)}, f32[1,1024]{1,0:T(1,128)S(1)}, u32[]{:S(2)}, u32[]{:S(2)}) collective-permute-start(f32[1,1024]{1,0:T(1,128)S(1)} %get-tuple-element.445), channel_id=1, source_target_pairs={{0,2},{2,0},{4,6},{6,4},{8,10},{10,8},{12,14},{14,12},{1,3},{3,1},... | collective-permute-start | bytes 12296 | tf_op jit(solution)/shard_map/ppermute | solution.py:188
  116.8 3.6 %collective-permute-start.31 = (f32[1,1024]{1,0:T(1,128)S(1)}, f32[1,1024]{1,0:T(1,128)S(1)}, u32[]{:S(2)}, u32[]{:S(2)}) collective-permute-start(f32[1,1024]{1,0:T(1,128)S(1)} %add.310), channel_id=1, source_target_pairs={{0,4},{2,6},{4,0},{6,2},{8,12},{10,14},{12,8},{14,10},{1,5},{3,7},... | collective-permute-start | bytes 12296 | tf_op jit(solution)/shard_map/ppermute | solution.py:188
  120.4 4.5 %collective-permute-start.32 = (f32[1,1024]{1,0:T(1,128)S(1)}, f32[1,1024]{1,0:T(1,128)S(1)}, u32[]{:S(2)}, u32[]{:S(2)}) collective-permute-start(f32[1,1024]{1,0:T(1,128)S(1)} %add.312), channel_id=1, source_target_pairs={{0,8},{2,10},{4,12},{6,14},{8,0},{10,2},{12,4},{14,6},{1,9},{3,11}... | collective-permute-start | bytes 12296 | tf_op jit(solution)/shard_map/ppermute | solution.py:188
  121.8 3.1 %collective-permute-start.33 = (f32[32,1024]{1,0:T(8,128)S(1)}, f32[32,1024]{1,0:T(8,128)S(1)}, u32[]{:S(2)}, u32[]{:S(2)}) collective-permute-start(f32[32,1024]{1,0:T(8,128)S(1)} %get-tuple-element.431.refs_0_), channel_id=1, source_target_pairs={{0,1},{1,0},{2,3},{3,2},{4,5},{5,4},{6,7},{7,6},{8,9},{9,8},{10,11... | collective-permute-start | bytes 393224 | tf_op jit(solution)/shard_map/ppermute | solution.py:185
  128.4 3.7 %collective-permute-start.35 = (f32[1,1152]{1,0:T(1,128)S(1)}, f32[1,1152]{1,0:T(1,128)S(1)}, u32[]{:S(2)}, u32[]{:S(2)}) collective-permute-start(f32[1,1152]{1,0:T(1,128)S(1)} %pad_maximum_fusion.2), channel_id=1, source_target_pairs={{0,2},{2,0},{4,6},{6,4},{8,10},{10,8},{12,14},{14,12},{1,3},{3,1},... | collective-permute-start | bytes 13832 | tf_op jit(solution)/shard_map/ppermute | solution.py:188
  132.1 3.7 %collective-permute-start.36 = (f32[1,1152]{1,0:T(1,128)S(1)}, f32[1,1152]{1,0:T(1,128)S(1)}, u32[]{:S(2)}, u32[]{:S(2)}) collective-permute-start(f32[1,1152]{1,0:T(1,128)S(1)} %fusion.40), channel_id=1, source_target_pairs={{0,4},{2,6},{4,0},{6,2},{8,12},{10,14},{12,8},{14,10},{1,5},{3,7},... | collective-permute-start | bytes 13832 | tf_op jit(solution)/shard_map/ppermute | solution.py:188
  135.7 4.5 %collective-permute-start.37 = (f32[1,1152]{1,0:T(1,128)S(1)}, f32[1,1152]{1,0:T(1,128)S(1)}, u32[]{:S(2)}, u32[]{:S(2)}) collective-permute-start(f32[1,1152]{1,0:T(1,128)S(1)} %add.317), channel_id=1, source_target_pairs={{0,8},{2,10},{4,12},{6,14},{8,0},{10,2},{12,4},{14,6},{1,9},{3,11}... | collective-permute-start | bytes 13832 | tf_op jit(solution)/shard_map/ppermute | solution.py:188
  141.2 3.7 %collective-permute-start.39 = (f32[1,1024]{1,0:T(1,128)S(1)}, f32[1,1024]{1,0:T(1,128)S(1)}, u32[]{:S(2)}, u32[]{:S(2)}) collective-permute-start(f32[1,1024]{1,0:T(1,128)S(1)} %get-tuple-element.486), channel_id=1, source_target_pairs={{0,2},{2,0},{4,6},{6,4},{8,10},{10,8},{12,14},{14,12},{1,3},{3,1},... | collective-permute-start | bytes 12296 | tf_op jit(solution)/shard_map/ppermute | solution.py:188
  144.9 3.6 %collective-permute-start.40 = (f32[1,1024]{1,0:T(1,128)S(1)}, f32[1,1024]{1,0:T(1,128)S(1)}, u32[]{:S(2)}, u32[]{:S(2)}) collective-permute-start(f32[1,1024]{1,0:T(1,128)S(1)} %add.320), channel_id=1, source_target_pairs={{0,4},{2,6},{4,0},{6,2},{8,12},{10,14},{12,8},{14,10},{1,5},{3,7},... | collective-permute-start | bytes 12296 | tf_op jit(solution)/shard_map/ppermute | solution.py:188
  148.5 4.5 %collective-permute-start.41 = (f32[1,1024]{1,0:T(1,128)S(1)}, f32[1,1024]{1,0:T(1,128)S(1)}, u32[]{:S(2)}, u32[]{:S(2)}) collective-permute-start(f32[1,1024]{1,0:T(1,128)S(1)} %add.322), channel_id=1, source_target_pairs={{0,8},{2,10},{4,12},{6,14},{8,0},{10,2},{12,4},{14,6},{1,9},{3,11}... | collective-permute-start | bytes 12296 | tf_op jit(solution)/shard_map/ppermute | solution.py:188
  149.9 3.1 %collective-permute-start.42 = (f32[32,1024]{1,0:T(8,128)S(1)}, f32[32,1024]{1,0:T(8,128)S(1)}, u32[]{:S(2)}, u32[]{:S(2)}) collective-permute-start(f32[32,1024]{1,0:T(8,128)S(1)} %get-tuple-element.472.refs_0_), channel_id=1, source_target_pairs={{0,1},{1,0},{2,3},{3,2},{4,5},{5,4},{6,7},{7,6},{8,9},{9,8},{10,11... | collective-permute-start | bytes 393224 | tf_op jit(solution)/shard_map/ppermute | solution.py:185
  156.5 3.7 %collective-permute-start.44 = (f32[1,1152]{1,0:T(1,128)S(1)}, f32[1,1152]{1,0:T(1,128)S(1)}, u32[]{:S(2)}, u32[]{:S(2)}) collective-permute-start(f32[1,1152]{1,0:T(1,128)S(1)} %pad_maximum_fusion.3), channel_id=1, source_target_pairs={{0,2},{2,0},{4,6},{6,4},{8,10},{10,8},{12,14},{14,12},{1,3},{3,1},... | collective-permute-start | bytes 13832 | tf_op jit(solution)/shard_map/ppermute | solution.py:188
  160.2 3.7 %collective-permute-start.45 = (f32[1,1152]{1,0:T(1,128)S(1)}, f32[1,1152]{1,0:T(1,128)S(1)}, u32[]{:S(2)}, u32[]{:S(2)}) collective-permute-start(f32[1,1152]{1,0:T(1,128)S(1)} %fusion.39), channel_id=1, source_target_pairs={{0,4},{2,6},{4,0},{6,2},{8,12},{10,14},{12,8},{14,10},{1,5},{3,7},... | collective-permute-start | bytes 13832 | tf_op jit(solution)/shard_map/ppermute | solution.py:188
  163.9 4.5 %collective-permute-start.46 = (f32[1,1152]{1,0:T(1,128)S(1)}, f32[1,1152]{1,0:T(1,128)S(1)}, u32[]{:S(2)}, u32[]{:S(2)}) collective-permute-start(f32[1,1152]{1,0:T(1,128)S(1)} %add.327), channel_id=1, source_target_pairs={{0,8},{2,10},{4,12},{6,14},{8,0},{10,2},{12,4},{14,6},{1,9},{3,11}... | collective-permute-start | bytes 13832 | tf_op jit(solution)/shard_map/ppermute | solution.py:188
  169.4 3.7 %collective-permute-start.48 = (f32[1,1024]{1,0:T(1,128)S(1)}, f32[1,1024]{1,0:T(1,128)S(1)}, u32[]{:S(2)}, u32[]{:S(2)}) collective-permute-start(f32[1,1024]{1,0:T(1,128)S(1)} %get-tuple-element.527), channel_id=1, source_target_pairs={{0,2},{2,0},{4,6},{6,4},{8,10},{10,8},{12,14},{14,12},{1,3},{3,1},... | collective-permute-start | bytes 12296 | tf_op jit(solution)/shard_map/ppermute | solution.py:188
  173.1 3.6 %collective-permute-start.49 = (f32[1,1024]{1,0:T(1,128)S(1)}, f32[1,1024]{1,0:T(1,128)S(1)}, u32[]{:S(2)}, u32[]{:S(2)}) collective-permute-start(f32[1,1024]{1,0:T(1,128)S(1)} %add.330), channel_id=1, source_target_pairs={{0,4},{2,6},{4,0},{6,2},{8,12},{10,14},{12,8},{14,10},{1,5},{3,7},... | collective-permute-start | bytes 12296 | tf_op jit(solution)/shard_map/ppermute | solution.py:188
  176.7 4.5 %collective-permute-start.50 = (f32[1,1024]{1,0:T(1,128)S(1)}, f32[1,1024]{1,0:T(1,128)S(1)}, u32[]{:S(2)}, u32[]{:S(2)}) collective-permute-start(f32[1,1024]{1,0:T(1,128)S(1)} %add.332), channel_id=1, source_target_pairs={{0,8},{2,10},{4,12},{6,14},{8,0},{10,2},{12,4},{14,6},{1,9},{3,11}... | collective-permute-start | bytes 12296 | tf_op jit(solution)/shard_map/ppermute | solution.py:188
  178.1 3.1 %collective-permute-start.51 = (f32[32,1024]{1,0:T(8,128)S(1)}, f32[32,1024]{1,0:T(8,128)S(1)}, u32[]{:S(2)}, u32[]{:S(2)}) collective-permute-start(f32[32,1024]{1,0:T(8,128)S(1)} %get-tuple-element.513.refs_0_), channel_id=1, source_target_pairs={{0,1},{1,0},{2,3},{3,2},{4,5},{5,4},{6,7},{7,6},{8,9},{9,8},{10,11... | collective-permute-start | bytes 393224 | tf_op jit(solution)/shard_map/ppermute | solution.py:185
  184.8 3.7 %collective-permute-start.53 = (f32[1,1152]{1,0:T(1,128)S(1)}, f32[1,1152]{1,0:T(1,128)S(1)}, u32[]{:S(2)}, u32[]{:S(2)}) collective-permute-start(f32[1,1152]{1,0:T(1,128)S(1)} %pad_maximum_fusion.4), channel_id=1, source_target_pairs={{0,2},{2,0},{4,6},{6,4},{8,10},{10,8},{12,14},{14,12},{1,3},{3,1},... | collective-permute-start | bytes 13832 | tf_op jit(solution)/shard_map/ppermute | solution.py:188
  188.5 13.8 %collective-permute-start.54 = (f32[1,1152]{1,0:T(1,128)S(1)}, f32[1,1152]{1,0:T(1,128)S(1)}, u32[]{:S(2)}, u32[]{:S(2)}) collective-permute-start(f32[1,1152]{1,0:T(1,128)S(1)} %fusion.38), channel_id=1, source_target_pairs={{0,4},{2,6},{4,0},{6,2},{8,12},{10,14},{12,8},{14,10},{1,5},{3,7},... | collective-permute-start | bytes 13832 | tf_op jit(solution)/shard_map/ppermute | solution.py:188
  202.2 4.5 %collective-permute-start.55 = (f32[1,1152]{1,0:T(1,128)S(1)}, f32[1,1152]{1,0:T(1,128)S(1)}, u32[]{:S(2)}, u32[]{:S(2)}) collective-permute-start(f32[1,1152]{1,0:T(1,128)S(1)} %add.337), channel_id=1, source_target_pairs={{0,8},{2,10},{4,12},{6,14},{8,0},{10,2},{12,4},{14,6},{1,9},{3,11}... | collective-permute-start | bytes 13832 | tf_op jit(solution)/shard_map/ppermute | solution.py:188
  207.8 3.7 %collective-permute-start.57 = (f32[1,1024]{1,0:T(1,128)S(1)}, f32[1,1024]{1,0:T(1,128)S(1)}, u32[]{:S(2)}, u32[]{:S(2)}) collective-permute-start(f32[1,1024]{1,0:T(1,128)S(1)} %get-tuple-element.568), channel_id=1, source_target_pairs={{0,2},{2,0},{4,6},{6,4},{8,10},{10,8},{12,14},{14,12},{1,3},{3,1},... | collective-permute-start | bytes 12296 | tf_op jit(solution)/shard_map/ppermute | solution.py:188
  211.5 3.6 %collective-permute-start.58 = (f32[1,1024]{1,0:T(1,128)S(1)}, f32[1,1024]{1,0:T(1,128)S(1)}, u32[]{:S(2)}, u32[]{:S(2)}) collective-permute-start(f32[1,1024]{1,0:T(1,128)S(1)} %add.340), channel_id=1, source_target_pairs={{0,4},{2,6},{4,0},{6,2},{8,12},{10,14},{12,8},{14,10},{1,5},{3,7},... | collective-permute-start | bytes 12296 | tf_op jit(solution)/shard_map/ppermute | solution.py:188
  215.1 4.5 %collective-permute-start.59 = (f32[1,1024]{1,0:T(1,128)S(1)}, f32[1,1024]{1,0:T(1,128)S(1)}, u32[]{:S(2)}, u32[]{:S(2)}) collective-permute-start(f32[1,1024]{1,0:T(1,128)S(1)} %add.342), channel_id=1, source_target_pairs={{0,8},{2,10},{4,12},{6,14},{8,0},{10,2},{12,4},{14,6},{1,9},{3,11}... | collective-permute-start | bytes 12296 | tf_op jit(solution)/shard_map/ppermute | solution.py:188
  216.5 3.1 %collective-permute-start.60 = (f32[32,1024]{1,0:T(8,128)S(1)}, f32[32,1024]{1,0:T(8,128)S(1)}, u32[]{:S(2)}, u32[]{:S(2)}) collective-permute-start(f32[32,1024]{1,0:T(8,128)S(1)} %get-tuple-element.554.refs_0_), channel_id=1, source_target_pairs={{0,1},{1,0},{2,3},{3,2},{4,5},{5,4},{6,7},{7,6},{8,9},{9,8},{10,11... | collective-permute-start | bytes 393224 | tf_op jit(solution)/shard_map/ppermute | solution.py:185
  223.2 3.7 %collective-permute-start.62 = (f32[1,1152]{1,0:T(1,128)S(1)}, f32[1,1152]{1,0:T(1,128)S(1)}, u32[]{:S(2)}, u32[]{:S(2)}) collective-permute-start(f32[1,1152]{1,0:T(1,128)S(1)} %pad_maximum_fusion.5), channel_id=1, source_target_pairs={{0,2},{2,0},{4,6},{6,4},{8,10},{10,8},{12,14},{14,12},{1,3},{3,1},... | collective-permute-start | bytes 13832 | tf_op jit(solution)/shard_map/ppermute | solution.py:188
  226.9 3.7 %collective-permute-start.63 = (f32[1,1152]{1,0:T(1,128)S(1)}, f32[1,1152]{1,0:T(1,128)S(1)}, u32[]{:S(2)}, u32[]{:S(2)}) collective-permute-start(f32[1,1152]{1,0:T(1,128)S(1)} %fusion.37), channel_id=1, source_target_pairs={{0,4},{2,6},{4,0},{6,2},{8,12},{10,14},{12,8},{14,10},{1,5},{3,7},... | collective-permute-start | bytes 13832 | tf_op jit(solution)/shard_map/ppermute | solution.py:188
  230.6 4.5 %collective-permute-start.64 = (f32[1,1152]{1,0:T(1,128)S(1)}, f32[1,1152]{1,0:T(1,128)S(1)}, u32[]{:S(2)}, u32[]{:S(2)}) collective-permute-start(f32[1,1152]{1,0:T(1,128)S(1)} %add.347), channel_id=1, source_target_pairs={{0,8},{2,10},{4,12},{6,14},{8,0},{10,2},{12,4},{14,6},{1,9},{3,11}... | collective-permute-start | bytes 13832 | tf_op jit(solution)/shard_map/ppermute | solution.py:188
  236.2 3.7 %collective-permute-start.66 = (f32[1,1024]{1,0:T(1,128)S(1)}, f32[1,1024]{1,0:T(1,128)S(1)}, u32[]{:S(2)}, u32[]{:S(2)}) collective-permute-start(f32[1,1024]{1,0:T(1,128)S(1)} %get-tuple-element.609), channel_id=1, source_target_pairs={{0,2},{2,0},{4,6},{6,4},{8,10},{10,8},{12,14},{14,12},{1,3},{3,1},... | collective-permute-start | bytes 12296 | tf_op jit(solution)/shard_map/ppermute | solution.py:188
  239.9 3.6 %collective-permute-start.67 = (f32[1,1024]{1,0:T(1,128)S(1)}, f32[1,1024]{1,0:T(1,128)S(1)}, u32[]{:S(2)}, u32[]{:S(2)}) collective-permute-start(f32[1,1024]{1,0:T(1,128)S(1)} %add.350), channel_id=1, source_target_pairs={{0,4},{2,6},{4,0},{6,2},{8,12},{10,14},{12,8},{14,10},{1,5},{3,7},... | collective-permute-start | bytes 12296 | tf_op jit(solution)/shard_map/ppermute | solution.py:188
  243.5 4.5 %collective-permute-start.68 = (f32[1,1024]{1,0:T(1,128)S(1)}, f32[1,1024]{1,0:T(1,128)S(1)}, u32[]{:S(2)}, u32[]{:S(2)}) collective-permute-start(f32[1,1024]{1,0:T(1,128)S(1)} %add.352), channel_id=1, source_target_pairs={{0,8},{2,10},{4,12},{6,14},{8,0},{10,2},{12,4},{14,6},{1,9},{3,11}... | collective-permute-start | bytes 12296 | tf_op jit(solution)/shard_map/ppermute | solution.py:188
  244.9 3.1 %collective-permute-start.69 = (f32[32,1024]{1,0:T(8,128)S(1)}, f32[32,1024]{1,0:T(8,128)S(1)}, u32[]{:S(2)}, u32[]{:S(2)}) collective-permute-start(f32[32,1024]{1,0:T(8,128)S(1)} %get-tuple-element.595.refs_0_), channel_id=1, source_target_pairs={{0,1},{1,0},{2,3},{3,2},{4,5},{5,4},{6,7},{7,6},{8,9},{9,8},{10,11... | collective-permute-start | bytes 393224 | tf_op jit(solution)/shard_map/ppermute | solution.py:185
  251.5 3.7 %collective-permute-start.71 = (f32[1,1152]{1,0:T(1,128)S(1)}, f32[1,1152]{1,0:T(1,128)S(1)}, u32[]{:S(2)}, u32[]{:S(2)}) collective-permute-start(f32[1,1152]{1,0:T(1,128)S(1)} %pad_maximum_fusion.6), channel_id=1, source_target_pairs={{0,2},{2,0},{4,6},{6,4},{8,10},{10,8},{12,14},{14,12},{1,3},{3,1},... | collective-permute-start | bytes 13832 | tf_op jit(solution)/shard_map/ppermute | solution.py:188
  255.2 3.7 %collective-permute-start.72 = (f32[1,1152]{1,0:T(1,128)S(1)}, f32[1,1152]{1,0:T(1,128)S(1)}, u32[]{:S(2)}, u32[]{:S(2)}) collective-permute-start(f32[1,1152]{1,0:T(1,128)S(1)} %fusion.36), channel_id=1, source_target_pairs={{0,4},{2,6},{4,0},{6,2},{8,12},{10,14},{12,8},{14,10},{1,5},{3,7},... | collective-permute-start | bytes 13832 | tf_op jit(solution)/shard_map/ppermute | solution.py:188
  258.9 4.5 %collective-permute-start.73 = (f32[1,1152]{1,0:T(1,128)S(1)}, f32[1,1152]{1,0:T(1,128)S(1)}, u32[]{:S(2)}, u32[]{:S(2)}) collective-permute-start(f32[1,1152]{1,0:T(1,128)S(1)} %add.357), channel_id=1, source_target_pairs={{0,8},{2,10},{4,12},{6,14},{8,0},{10,2},{12,4},{14,6},{1,9},{3,11}... | collective-permute-start | bytes 13832 | tf_op jit(solution)/shard_map/ppermute | solution.py:188
  265.3 3.6 %collective-permute-start.76 = (f32[1,1024]{1,0:T(1,128)S(1)}, f32[1,1024]{1,0:T(1,128)S(1)}, u32[]{:S(2)}, u32[]{:S(2)}) collective-permute-start(f32[1,1024]{1,0:T(1,128)S(1)} %get-tuple-element.656), channel_id=1, source_target_pairs={{0,2},{2,0},{4,6},{6,4},{8,10},{10,8},{12,14},{14,12},{1,3},{3,1},... | collective-permute-start | bytes 12296 | tf_op jit(solution)/shard_map/ppermute | solution.py:188
  268.9 3.6 %collective-permute-start.77 = (f32[1,1024]{1,0:T(1,128)S(1)}, f32[1,1024]{1,0:T(1,128)S(1)}, u32[]{:S(2)}, u32[]{:S(2)}) collective-permute-start(f32[1,1024]{1,0:T(1,128)S(1)} %add.360), channel_id=1, source_target_pairs={{0,4},{2,6},{4,0},{6,2},{8,12},{10,14},{12,8},{14,10},{1,5},{3,7},... | collective-permute-start | bytes 12296 | tf_op jit(solution)/shard_map/ppermute | solution.py:188
  272.5 4.5 %collective-permute-start.78 = (f32[1,1024]{1,0:T(1,128)S(1)}, f32[1,1024]{1,0:T(1,128)S(1)}, u32[]{:S(2)}, u32[]{:S(2)}) collective-permute-start(f32[1,1024]{1,0:T(1,128)S(1)} %add.362), channel_id=1, source_target_pairs={{0,8},{2,10},{4,12},{6,14},{8,0},{10,2},{12,4},{14,6},{1,9},{3,11}... | collective-permute-start | bytes 12296 | tf_op jit(solution)/shard_map/ppermute | solution.py:188
  281.8 3.5 %collective-permute-start.80 = (f32[1,128]{1,0:T(1,128)S(1)}, f32[1,128]{1,0:T(1,128)S(1)}, u32[]{:S(2)}, u32[]{:S(2)}) collective-permute-start(f32[1,128]{1,0:T(1,128)S(1)} %add.364), channel_id=1, source_target_pairs={{0,2},{2,0},{4,6},{6,4},{8,10},{10,8},{12,14},{14,12},{1,3},{3,1},... | collective-permute-start | bytes 1544 | tf_op jit(solution)/shard_map/ppermute | solution.py:188
  285.3 3.5 %collective-permute-start.81 = (f32[1,128]{1,0:T(1,128)S(1)}, f32[1,128]{1,0:T(1,128)S(1)}, u32[]{:S(2)}, u32[]{:S(2)}) collective-permute-start(f32[1,128]{1,0:T(1,128)S(1)} %add.365), channel_id=1, source_target_pairs={{0,4},{2,6},{4,0},{6,2},{8,12},{10,14},{12,8},{14,10},{1,5},{3,7},... | collective-permute-start | bytes 1544 | tf_op jit(solution)/shard_map/ppermute | solution.py:188
  288.8 4.4 %collective-permute-start.82 = (f32[1,128]{1,0:T(1,128)S(1)}, f32[1,128]{1,0:T(1,128)S(1)}, u32[]{:S(2)}, u32[]{:S(2)}) collective-permute-start(f32[1,128]{1,0:T(1,128)S(1)} %add.366), channel_id=1, source_target_pairs={{0,8},{2,10},{4,12},{6,14},{8,0},{10,2},{12,4},{14,6},{1,9},{3,11}... | collective-permute-start | bytes 1544 | tf_op jit(solution)/shard_map/ppermute | solution.py:188
  (40 other events, 93.0 us)
